TPU v7x, 32 devices: a whole 2x2x4 slice. The times are simulated.
32 devices in a mesh: bx: 2 (over x), by: 4 (over z), bz: 4 (over y, core).
Axes of the slice: x: 2, y: 2, z: 4, core: 2. Of those that a mesh axis runs over, the one named last changes fastest.
Arguments:
- estimate: float32 [32, 64, 512], P('bx', 'by', 'bz'), may hold values from 0.5 to 2
- raw_views: float32 [6, 32, 64, 512], P(None, 'bx', 'by', 'bz'), may hold values from 0.25 to 4
- psf: float32 [6, 3, 31], replicated, may hold values from 0.05 to 1
- offsets: int32 [6, 3], replicated, may hold values from -8 to 8, as said below
- coverage: int32 [6, 2, 4, 4], P(None, 'bx', 'by', 'bz'), may hold values from 0 to 1, as said below
Outputs:
- restored: float32 [32, 64, 512], P('bx', 'by', 'bz')
Inputs may be any that keep to these rules, and one draw needn't show every extreme that they name: `offsets`: one view has first component exactly 8 and the next view (cyclically) third component exactly -8. `coverage`: every output block is covered by at least one view.
All inputs are finite; a program needn't handle non-finite values.
Results may differ from a plain program's by a relative error of at most 0.0001.
Values sent between devices are 32-bit elements; how exact they have to be, the bound alone decides.
A program may use at most 128 MiB of HBM per device.

v0:
```python
import functools

import jax
import jax.numpy as jnp
from jax import lax
from jax.experimental import pallas as pl
from jax.experimental.pallas import tpu as pltpu
from jax.sharding import PartitionSpec as P

F32 = jnp.float32
BF16 = jnp.bfloat16
MESH = pl.DeviceIdType.MESH
OFF = 8
TAPS = 31
REACH = 15
VIEWS = 6
SX = 16
SY = 16
SZ = 128
XY = SX * SY
LOW, LOW_COV, OWN, OWN_COV, HIGH, HIGH_COV, ROWS = 0, 16, 24, 152, 160, 176, 256


def split(value):
    high = value.astype(BF16)
    return high, (value - high.astype(F32)).astype(BF16)


def dot(a, b):
    return jnp.dot(a, b, preferred_element_type=F32)


def dot3(a_high, a_low, b_high, b_low):
    return dot(a_high, b_high) + (dot(a_high, b_low) + dot(a_low, b_high))


def iota(shape, dim):
    return lax.broadcasted_iota(jnp.int32, shape, dim)


def kernel(
    counts, est, raw, psf_s, psf_v, offsets, coverage, out,
    wide, wide_h, wide_l, rx, ry, rz, kn,
    kron_h, kron_l, kront_h, kront_l, fz_h, fz_l, bz_h, bz_l,
    blurred, back_h, back_l, spread, from_z, from_y, from_x, weights, send, recv,
):
    nx, ny, nz = counts
    xslots = 2 if nx == 2 else 3
    group = xslots * XY
    lanes = 3 * group
    ix, iy, iz = lax.axis_index("bx"), lax.axis_index("by"), lax.axis_index("bz")
    where = {"bx": (ix, nx), "by": (iy, ny), "bz": (iz, nz)}
    has_left = {name: i > 0 for name, (i, n) in where.items()}
    has_right = {name: i < n - 1 for name, (i, n) in where.items()}
    x_shift = [0, 1 - 2 * ix] if nx == 2 else [0, -1, 1]
    y_shift = [0, -1, 1]
    x_left_slot = 1
    x_right_slot = 1 if nx == 2 else 2

    def to_left(axis, index, src, dst):
        return axis, True, pltpu.make_async_remote_copy(
            src_ref=src, dst_ref=dst, send_sem=send.at[index], recv_sem=recv.at[index],
            device_id={axis: where[axis][0] - 1}, device_id_type=MESH,
        )

    def to_right(axis, index, src, dst):
        return axis, False, pltpu.make_async_remote_copy(
            src_ref=src, dst_ref=dst, send_sem=send.at[index], recv_sem=recv.at[index],
            device_id={axis: where[axis][0] + 1}, device_id_type=MESH,
        )

    def start(copies):
        for axis, left, copy in copies:
            @pl.when(has_left[axis] if left else has_right[axis])
            def _():
                copy.start()

    def arrive(copies):
        for axis, left, copy in copies:
            @pl.when(has_right[axis] if left else has_left[axis])
            def _():
                copy.wait_recv()

    def sent(copies):
        for axis, left, copy in copies:
            @pl.when(has_left[axis] if left else has_right[axis])
            def _():
                copy.wait_send()

    def absent(axis, left, ref, index):
        @pl.when(jnp.logical_not(has_left[axis] if left else has_right[axis]))
        def _():
            ref[index] = jnp.zeros(ref.at[index].shape, ref.dtype)

    full = slice(None)
    own_rows = slice(OWN, OWN_COV + 8)

    wide[OWN:OWN_COV, 0:XY] = est[...].reshape(XY, SZ).T
    cov_rows = jnp.zeros((8, XY), F32)
    for view in range(VIEWS):
        value = coverage[view, 0, 0, 0].astype(F32)
        cov_rows = jnp.where(iota((8, XY), 0) == view, value, cov_rows)
    wide[OWN_COV : OWN_COV + 8, 0:XY] = cov_rows
    wide[HIGH_COV + 8 : ROWS, :] = jnp.zeros((ROWS - HIGH_COV - 8, lanes), F32)
    if nx > 2:
        absent("bx", True, wide, (own_rows, slice(XY, 2 * XY)))
        absent("bx", False, wide, (own_rows, slice(2 * XY, 3 * XY)))
    absent("by", True, wide, (own_rows, slice(group, 2 * group)))
    absent("by", False, wide, (own_rows, slice(2 * group, 3 * group)))
    absent("bz", True, wide, (slice(LOW, OWN), full))
    absent("bz", False, wide, (slice(HIGH, HIGH_COV + 8), full))
    absent("bx", True, rx, (full, slice(0, 8), full, full))
    absent("bx", False, rx, (full, slice(24, 32), full, full))
    absent("by", True, ry, (full, full, slice(0, 8), full))
    absent("by", False, ry, (full, full, slice(24, 32), full))
    absent("bz", True, rz, (full, slice(0, 8), full))
    absent("bz", False, rz, (full, slice(136, 144), full))
    rx[:, 8:24] = raw[...]

    barrier = pltpu.get_barrier_semaphore()
    for axis, (i, n) in where.items():
        @pl.when(has_left[axis])
        def _():
            pl.semaphore_signal(barrier, inc=1, device_id={axis: i - 1}, device_id_type=MESH)

        @pl.when(has_right[axis])
        def _():
            pl.semaphore_signal(barrier, inc=1, device_id={axis: i + 1}, device_id_type=MESH)
    degree = sum(
        (has_left[axis].astype(jnp.int32) + has_right[axis].astype(jnp.int32) for axis in where),
        jnp.int32(0),
    )
    pl.semaphore_wait(barrier, degree)

    def lane_slot(slot):
        return slice(slot * XY, (slot + 1) * XY)

    est_x = [
        to_left("bx", 0, wide.at[own_rows, 0:XY], wide.at[own_rows, lane_slot(x_right_slot)]),
        to_right("bx", 1, wide.at[own_rows, 0:XY], wide.at[own_rows, lane_slot(x_left_slot)]),
    ]
    est_y = [
        to_left("by", 2, wide.at[own_rows, 0:group], wide.at[own_rows, 2 * group : 3 * group]),
        to_right("by", 3, wide.at[own_rows, 0:group], wide.at[own_rows, group : 2 * group]),
    ]
    est_z = [
        to_left("bz", 4, wide.at[OWN : OWN + 16], wide.at[HIGH : HIGH + 16]),
        to_left("bz", 5, wide.at[OWN_COV : OWN_COV + 8], wide.at[HIGH_COV : HIGH_COV + 8]),
        to_right("bz", 6, wide.at[OWN_COV - 16 : OWN_COV + 8], wide.at[LOW : LOW + 24]),
    ]
    raw_x = [
        to_left("bx", 7, rx.at[:, 8:16], rx.at[:, 24:32]),
        to_right("bx", 8, rx.at[:, 16:24], rx.at[:, 0:8]),
    ]
    raw_y = [
        to_left("by", 9, ry.at[:, :, 8:16], ry.at[:, :, 24:32]),
        to_right("by", 10, ry.at[:, :, 16:24], ry.at[:, :, 0:8]),
    ]
    raw_z = [
        to_left("bz", 11, rz.at[:, 8:16], rz.at[:, 136:144]),
        to_right("bz", 12, rz.at[:, 128:136], rz.at[:, 0:8]),
    ]

    def toeplitz(view, axis, places, total):
        result = [jnp.zeros(place.shape, F32) for place in places]
        for tap in range(TAPS):
            value = psf_s[view, axis, tap]
            result = [jnp.where(p == tap, value, r) for p, r in zip(places, result)]
        return [r / jnp.full(r.shape, total, F32) for r in result]

    def build(first, last):
        @pl.loop(first, last)
        def _(view):
            totals = []
            for axis in range(3):
                total = psf_s[view, axis, 0]
                for tap in range(1, TAPS):
                    total = total + psf_s[view, axis, tap]
                totals.append(total)
            row, lane = iota((16, XY), 0), iota((16, XY), 1)
            lane_x, lane_y = lane // SY, lane % SY
            x_to = [REACH + SX * d + lane_x - row for d in x_shift]
            x_from = [REACH + SX * d + row - lane_x for d in x_shift]
            y_to = [REACH + SY * d + lane_y - row for d in y_shift]
            y_from = [REACH + SY * d + row - lane_y for d in y_shift]
            xs = toeplitz(view, 0, x_to + x_from, totals[0])
            ys = toeplitz(view, 1, y_to + y_from, totals[1])
            for y in range(3):
                for x in range(xslots):
                    base = y * group + x * XY
                    for i in range(16):
                        high, low = split(ys[y] * xs[x][i : i + 1, :])
                        kron_h[view, i * 16 : (i + 1) * 16, base : base + XY] = high
                        kron_l[view, i * 16 : (i + 1) * 16, base : base + XY] = low
                        high, low = split(ys[3 + y] * xs[xslots + x][i : i + 1, :])
                        kront_h[view, base + i * 16 : base + (i + 1) * 16, :] = high
                        kront_l[view, base + i * 16 : base + (i + 1) * 16, :] = low
            row, lane = iota((SZ, ROWS), 0), iota((SZ, ROWS), 1)
            place = jnp.where(
                lane < LOW_COV, lane - 16,
                jnp.where(
                    (lane >= OWN) & (lane < OWN_COV), lane - OWN,
                    jnp.where((lane >= HIGH) & (lane < HIGH_COV), lane - HIGH + SZ, 10000),
                ),
            )
            (matrix,) = toeplitz(view, 2, [REACH + place - row], totals[2])
            fz_h[view], fz_l[view] = split(matrix)
            row, lane = iota((SZ + 32, SZ), 0), iota((SZ + 32, SZ), 1)
            (matrix,) = toeplitz(view, 2, [REACH - 16 + row - lane], totals[2])
            bz_h[view], bz_l[view] = split(matrix)

    start(est_x)
    start(raw_x)
    kn[...] = jnp.zeros(kn.shape, F32)
    for axis in range(3):
        values = psf_v[:, axis, :]
        kn[axis, 0:VIEWS, 0:TAPS] = values / jnp.sum(values, axis=1, keepdims=True)
    arrive(est_x)
    start(est_y)
    build(0, 3)
    arrive(raw_x)

    @pl.loop(0, VIEWS)
    def _(view):
        ry[view, :, 8:24, :] = rx[view, pl.ds(OFF + offsets[view, 0], SX), :, :]

    start(raw_y)
    arrive(est_y)
    start(est_z)
    build(3, VIEWS)
    arrive(est_z)

    highest = lax.Precision.HIGHEST
    tap, lane = iota((128, XY), 0), iota((128, XY), 1)
    lane_x, lane_y = lane // SY, lane % SY

    def factor(axis, position, shift, size):
        cell = position + REACH - tap[:, : position.shape[1]] - shift * size
        inside = ((cell >= 0) & (cell < size)).astype(F32)
        return jnp.dot(kn[axis], inside, precision=highest, preferred_element_type=F32)

    factor_x = [factor(0, lane_x, d, SX) for d in x_shift]
    factor_y = [factor(1, lane_y, d, SY) for d in y_shift]
    factor_z = [factor(2, lane[:, :SZ], d, SZ) for d in (-1, 0, 1)]
    rows = []
    for base in (LOW_COV, OWN_COV, HIGH_COV):
        total = jnp.zeros((8, XY), F32)
        for y in range(3):
            part = jnp.zeros((8, XY), F32)
            for x in range(xslots):
                first = y * group + x * XY
                part = part + wide[base : base + 8, first : first + XY] * factor_x[x]
            total = total + part * factor_y[y]
        rows.append(total)
    weights[...] = jnp.dot(
        jnp.concatenate(factor_z, axis=0).T, jnp.concatenate(rows, axis=0),
        precision=highest, preferred_element_type=F32,
    )

    wide_h[...], wide_l[...] = split(wide[...])

    @pl.loop(0, VIEWS)
    def _(view):
        total = jnp.zeros((SZ, XY), F32)
        for y in range(3):
            cut = slice(y * group, (y + 1) * group)
            high, low = split(dot3(fz_h[view], fz_l[view], wide_h[:, cut], wide_l[:, cut]))
            total = total + dot3(high, low, kront_h[view, cut, :], kront_l[view, cut, :])
        blurred[view] = total

    arrive(raw_y)

    @pl.loop(0, VIEWS)
    def _(view):
        turn = lax.rem(32 - OFF - offsets[view, 1], 32)
        shifted = pltpu.roll(ry[view], turn, 1)[:, 0:SY, :]
        rz[view, 8:136, :] = shifted.reshape(XY, SZ).T

    start(raw_z)
    arrive(raw_z)

    @pl.loop(0, VIEWS)
    def _(view):
        turn = lax.rem(SZ + 16 - OFF - offsets[view, 2], SZ + 16)
        observed = pltpu.roll(rz[view], turn, 0)[0:SZ, :]
        mask = coverage[view, 0, 0, 0].astype(F32)
        high, low = split(mask * observed / blurred[view])
        rows_of = pl.ds(pl.multiple_of(view * SZ, SZ), SZ)
        for y in range(3):
            cut = slice(y * group, (y + 1) * group)
            part = dot3(high, low, kron_h[view, :, cut], kron_l[view, :, cut])
            back_h[rows_of, cut], back_l[rows_of, cut] = split(part)

    for y in range(3):
        cut = slice(y * group, (y + 1) * group)
        total = jnp.zeros((SZ + 32, group), F32)
        for view in range(VIEWS):
            rows_of = slice(view * SZ, (view + 1) * SZ)
            total = total + dot3(bz_h[view], bz_l[view], back_h[rows_of, cut], back_l[rows_of, cut])
        spread[:, cut] = total

    back_z = [
        to_left("bz", 13, spread.at[0:16], from_z.at[1]),
        to_right("bz", 14, spread.at[SZ + 16 : SZ + 32], from_z.at[0]),
    ]
    absent("bz", True, from_z, (0, full, full))
    absent("bz", False, from_z, (1, full, full))
    absent("by", True, from_y, (0, full, full))
    absent("by", False, from_y, (1, full, full))
    absent("bx", True, from_x, (0, full, full))
    absent("bx", False, from_x, (1, full, full))
    start(back_z)
    arrive(back_z)
    spread[16:32, :] = spread[16:32, :] + from_z[0]
    spread[SZ : SZ + 16, :] = spread[SZ : SZ + 16, :] + from_z[1]
    mid = slice(16, SZ + 16)
    back_y = [
        to_left("by", 15, spread.at[mid, group : 2 * group], from_y.at[1]),
        to_right("by", 16, spread.at[mid, 2 * group : 3 * group], from_y.at[0]),
    ]
    start(back_y)
    arrive(back_y)
    spread[mid, 0:group] = spread[mid, 0:group] + from_y[0] + from_y[1]
    back_x = [
        to_left("bx", 17, spread.at[mid, lane_slot(x_left_slot)], from_x.at[1]),
        to_right("bx", 18, spread.at[mid, lane_slot(x_right_slot)], from_x.at[0]),
    ]
    start(back_x)
    arrive(back_x)
    total = spread[mid, 0:XY] + from_x[0] + from_x[1]
    restored = wide[OWN:OWN_COV, 0:XY] * total / weights[...]
    out[...] = restored.T.reshape(SX, SY, SZ)
    for copies in (est_x, est_y, est_z, raw_x, raw_y, raw_z, back_z, back_y, back_x):
        sent(copies)


def on_device(counts, estimate, raw_views, psf, offsets, coverage):
    xslots = 2 if counts[0] == 2 else 3
    group = xslots * XY
    lanes = 3 * group
    vmem = pl.BlockSpec(memory_space=pltpu.VMEM)
    smem = pl.BlockSpec(memory_space=pltpu.SMEM)
    return pl.pallas_call(
        functools.partial(kernel, counts),
        out_shape=jax.ShapeDtypeStruct(estimate.shape, F32),
        in_specs=[vmem, vmem, smem, vmem, smem, smem],
        out_specs=vmem,
        scratch_shapes=[
            pltpu.VMEM((ROWS, lanes), F32),
            pltpu.VMEM((ROWS, lanes), BF16),
            pltpu.VMEM((ROWS, lanes), BF16),
            pltpu.VMEM((VIEWS, 32, SY, SZ), F32),
            pltpu.VMEM((VIEWS, SX, 32, SZ), F32),
            pltpu.VMEM((VIEWS, SZ + 16, XY), F32),
            pltpu.VMEM((3, 8, 128), F32),
            pltpu.VMEM((VIEWS, XY, lanes), BF16),
            pltpu.VMEM((VIEWS, XY, lanes), BF16),
            pltpu.VMEM((VIEWS, lanes, XY), BF16),
            pltpu.VMEM((VIEWS, lanes, XY), BF16),
            pltpu.VMEM((VIEWS, SZ, ROWS), BF16),
            pltpu.VMEM((VIEWS, SZ, ROWS), BF16),
            pltpu.VMEM((VIEWS, SZ + 32, SZ), BF16),
            pltpu.VMEM((VIEWS, SZ + 32, SZ), BF16),
            pltpu.VMEM((VIEWS, SZ, XY), F32),
            pltpu.VMEM((VIEWS * SZ, lanes), BF16),
            pltpu.VMEM((VIEWS * SZ, lanes), BF16),
            pltpu.VMEM((SZ + 32, lanes), F32),
            pltpu.VMEM((2, 16, lanes), F32),
            pltpu.VMEM((2, SZ, group), F32),
            pltpu.VMEM((2, SZ, XY), F32),
            pltpu.VMEM((SZ, XY), F32),
            pltpu.SemaphoreType.DMA((19,)),
            pltpu.SemaphoreType.DMA((19,)),
        ],
        compiler_params=pltpu.CompilerParams(
            collective_id=0, has_side_effects=True, vmem_limit_bytes=56 * 1024 * 1024
        ),
    )(estimate, raw_views, psf, psf, offsets, coverage)


def solution(mesh):
    counts = (mesh.shape["bx"], mesh.shape["by"], mesh.shape["bz"])
    return jax.shard_map(
        functools.partial(on_device, counts),
        mesh=mesh,
        in_specs=(
            P("bx", "by", "bz"),
            P(None, "bx", "by", "bz"),
            P(),
            P(),
            P(None, "bx", "by", "bz"),
        ),
        out_specs=P("bx", "by", "bz"),
        check_vma=False,
    )
```

profile of v0, /device:TPU:1, one launch (start us, length us, event | category | flops | bytes accessed | tf_op | source)
XLA Modules:
  0.0 54.7 jit_solution(6830415070171320858)
XLA Ops:
  0.0 0.0 copy-start
  0.0 1.3 %copy.7.coverage = s32[6,1,1,1]{3,2,1,0:T(1,128)} copy(s32[6,1,1,1]{0,3,2,1:T(1,128)} %param.9) | data formatting | bytes 48 | tf_op args[4]
  1.3 0.0 copy-done
  1.3 0.7 %copy.6.offsets = s32[6,3]{1,0:T(8,128)} copy(s32[6,3]{0,1:T(4,128)S(1)} %copy-done) | data formatting | bytes 144 | tf_op args[3]
  2.0 51.1 %shard_map.55 = f32[16,16,128]{2,1,0:T(8,128)} custom-call(f32[16,16,128]{2,1,0:T(8,128)} %est.1, f32[6,16,16,128]{3,2,1,0:T(8,128)} %raw.1, f32[6,3,31]{2,1,0:T(4,128)} %psf_v.1, f32[6,3,31]{2,1,0:T(4,128)} %psf_v.1, s32[6,3]{1,0:T(8,128)} %copy.6.offsets, s32[6,1,1,1]{3,2,1,0:T(1,128)} %copy.7.coverage), custom_call_target="tpu_custom_call" | custom-call | tf_op jit(solution)/shard_map/pallas_call | solution.py:343
  53.1 1.6 %copy.9 = f32[16,16,128]{2,1,0:T(8,128)} copy(f32[16,16,128]{2,1,0:T(8,128)} %shard_map.55) | data formatting | bytes 262144
Async XLA Ops:
  0.0 1.3 %copy-start = (s32[6,3]{0,1:T(4,128)S(1)}, s32[6,3]{0,1:T(4,128)}, u32[]{:S(2)}) copy-start(s32[6,3]{0,1:T(4,128)} %param.8) | copy-start | bytes 220
where the time goes:
time: 54.9 us; the launch traced here: 54.7 us
  Pallas kernels  51.1 us (93%)
  local copies, waits for them, and re-layouts  3.59 us (7%)
    pallas_call x1, Pallas kernels, on_device(): pl.pallas_call(functools.partial(kernel, counts), out_shape=jax.ShapeDtyp...  51.1 us
    unnamed x5, local copies, waits for them, and re-layouts  3.59 us

commit v1 on v0

v1 whole, which is shorter than its diff:
```python
import functools

import jax
import jax.numpy as jnp
from jax import lax
from jax.experimental import pallas as pl
from jax.experimental.pallas import tpu as pltpu
from jax.sharding import PartitionSpec as P

F32 = jnp.float32
BF16 = jnp.bfloat16
MESH = pl.DeviceIdType.MESH
OFF = 8
TAPS = 31
REACH = 15
VIEWS = 6
SEMAPHORES = 48
SX = 16
SY = 16
SZ = 128
XY = SX * SY
HIGH, GAP, LOW, ROWS = SZ, SZ + 16, 240, 256
WIDE = SZ + 32


def split(value):
    high = value.astype(BF16)
    return high, (value - high.astype(F32)).astype(BF16)


def dot(a, b):
    return jnp.dot(a, b, preferred_element_type=F32)


def iota(shape, dim):
    return lax.broadcasted_iota(jnp.int32, shape, dim)


def dot3(stack, b_high, b_low):
    half = stack.shape[0] // 2
    both = dot(stack, b_high)
    return both[:half] + (both[half:] + dot(stack[:half], b_low))


def kernel(
    counts, est, raw, psf_s, psf_v, offsets, coverage, out,
    wide, wide_h, wide_l, cov, rx_a, rx_b, ry_a, ry_b, rz, kn, knz, scale,
    kron_h, kron_l, kront_h, kront_l, fz, bz,
    blurred, ratio, back_h, back_l, spread, from_x, from_y, from_z, weights, send, recv,
):
    nx, ny, nz = counts
    xslots = 2 if nx == 2 else 3
    group = 3 * XY
    lanes = xslots * group
    ix, iy, iz = lax.axis_index("bx"), lax.axis_index("by"), lax.axis_index("bz")
    where = {"bx": (ix, nx), "by": (iy, ny), "bz": (iz, nz)}
    has_left = {name: i > 0 for name, (i, n) in where.items()}
    has_right = {name: i < n - 1 for name, (i, n) in where.items()}
    x_shift = [0, 1 - 2 * ix] if nx == 2 else [0, -1, 1]
    y_shift = [0, -1, 1]
    x_left_slot = 1
    x_right_slot = 1 if nx == 2 else 2
    used = iter(range(SEMAPHORES))

    def to_side(axis, left, src, dst):
        index = next(used)
        return axis, left, pltpu.make_async_remote_copy(
            src_ref=src, dst_ref=dst, send_sem=send.at[index], recv_sem=recv.at[index],
            device_id={axis: where[axis][0] + (-1 if left else 1)}, device_id_type=MESH,
        )

    def to_left(axis, src, dst):
        return to_side(axis, True, src, dst)

    def to_right(axis, src, dst):
        return to_side(axis, False, src, dst)

    def start(copies):
        for axis, left, copy in copies:
            @pl.when(has_left[axis] if left else has_right[axis])
            def _():
                copy.start()

    def arrive(copies):
        for axis, left, copy in copies:
            @pl.when(has_right[axis] if left else has_left[axis])
            def _():
                copy.wait_recv()

    def sent(copies):
        for axis, left, copy in copies:
            @pl.when(has_left[axis] if left else has_right[axis])
            def _():
                copy.wait_send()

    def absent(axis, left, ref, index):
        @pl.when(jnp.logical_not(has_left[axis] if left else has_right[axis]))
        def _():
            ref[index] = jnp.zeros(ref.at[index].shape, ref.dtype)

    def block(x, y):
        return slice((3 * x + y) * XY, (3 * x + y + 1) * XY)

    full = slice(None)
    own = slice(0, SZ)

    barrier = pltpu.get_barrier_semaphore()
    for axis, (i, n) in where.items():
        @pl.when(has_left[axis])
        def _():
            pl.semaphore_signal(barrier, inc=1, device_id={axis: i - 1}, device_id_type=MESH)

        @pl.when(has_right[axis])
        def _():
            pl.semaphore_signal(barrier, inc=1, device_id={axis: i + 1}, device_id_type=MESH)

    wide[own, block(0, 0)] = est[...].reshape(XY, SZ).T
    cov_rows = jnp.zeros((8, SZ), F32)
    for view in range(VIEWS):
        value = coverage[0, view].astype(F32)
        cov_rows = jnp.where(iota((8, SZ), 0) == view, value, cov_rows)
    cov[1, 0, 0] = cov_rows

    degree = sum(
        (has_left[axis].astype(jnp.int32) + has_right[axis].astype(jnp.int32) for axis in where),
        jnp.int32(0),
    )
    pl.semaphore_wait(barrier, degree)

    half = VIEWS // 2
    first, last = slice(0, half), slice(half, VIEWS)
    est_x = [
        to_left("bx", wide.at[own, block(0, 0)], wide.at[own, block(x_right_slot, 0)]),
        to_right("bx", wide.at[own, block(0, 0)], wide.at[own, block(x_left_slot, 0)]),
        to_left("bx", cov.at[1, 0, 0], cov.at[1, 0, x_right_slot]),
        to_right("bx", cov.at[1, 0, 0], cov.at[1, 0, x_left_slot]),
    ]
    est_y = [
        [
            to_left("by", wide.at[own, block(x, 0)], wide.at[own, block(x, 2)]),
            to_right("by", wide.at[own, block(x, 0)], wide.at[own, block(x, 1)]),
        ]
        for x in range(xslots)
    ]
    cov_y = [
        to_left("by", cov.at[1, 0], cov.at[1, 2]),
        to_right("by", cov.at[1, 0], cov.at[1, 1]),
    ]
    est_z = [
        to_left("bz", wide.at[0:16], wide.at[HIGH:GAP]),
        to_right("bz", wide.at[SZ - 16 : SZ], wide.at[LOW:ROWS]),
        to_left("bz", cov.at[1], cov.at[2]),
        to_right("bz", cov.at[1], cov.at[0]),
    ]
    raw_ax = [
        to_left("bx", raw.at[first, 0:8], rx_a.at[:, 24:32]),
        to_right("bx", raw.at[first, 8:16], rx_a.at[:, 0:8]),
    ]
    raw_ay = [
        to_left("by", ry_a.at[:, :, 8:16], ry_a.at[:, :, 24:32]),
        to_right("by", ry_a.at[:, :, 16:24], ry_a.at[:, :, 0:8]),
    ]
    raw_by = [
        to_left("by", raw.at[last, :, 0:8], ry_b.at[:, :, 24:32]),
        to_right("by", raw.at[last, :, 8:16], ry_b.at[:, :, 0:8]),
    ]
    raw_bx = [
        to_left("bx", rx_b.at[:, 8:16], rx_b.at[:, 24:32]),
        to_right("bx", rx_b.at[:, 16:24], rx_b.at[:, 0:8]),
    ]
    raw_z = [
        to_left("bz", rz.at[:, 8:16], rz.at[:, 136:144]),
        to_right("bz", rz.at[:, 128:136], rz.at[:, 0:8]),
    ]

    start(est_x)
    start(est_y[0])
    start(raw_ax)
    start(raw_by)

    wide[GAP:LOW, :] = jnp.zeros((LOW - GAP, lanes), F32)
    if nx > 2:
        for left, slot in ((True, x_left_slot), (False, x_right_slot)):
            absent("bx", left, wide, (own, block(slot, 0)))
            absent("bx", left, cov, (1, 0, slot, full, full))
    for left, slot in ((True, 1), (False, 2)):
        for x in range(xslots):
            absent("by", left, wide, (own, block(x, slot)))
        absent("by", left, cov, (1, slot, full, full, full))
    absent("bz", True, wide, (slice(LOW, ROWS), full))
    absent("bz", False, wide, (slice(HIGH, GAP), full))
    absent("bz", True, cov, (0, full, full, full, full))
    absent("bz", False, cov, (2, full, full, full, full))
    for rx, ry in ((rx_a, ry_a), (rx_b, ry_b)):
        absent("bx", True, rx, (full, slice(0, 8), full, full))
        absent("bx", False, rx, (full, slice(24, 32), full, full))
        absent("by", True, ry, (full, full, slice(0, 8), full))
        absent("by", False, ry, (full, full, slice(24, 32), full))
    absent("bz", True, rz, (full, slice(0, 8), full))
    absent("bz", False, rz, (full, slice(136, 144), full))
    absent("bz", True, from_z, (0, full, full))
    absent("bz", False, from_z, (1, full, full))
    absent("by", True, from_y, (0, full, full, full))
    absent("by", False, from_y, (1, full, full, full))
    absent("bx", True, from_x, (0, full, full))
    absent("bx", False, from_x, (1, full, full))
    rx_a[:, 8:24] = raw[first]
    ry_b[:, :, 8:24] = raw[last]

    kn[...] = jnp.zeros(kn.shape, F32)
    for axis in range(3):
        values = psf_v[:, axis, :]
        total = jnp.sum(values, axis=1, keepdims=True)
        kn[axis, 0:VIEWS, 0:TAPS] = values / total
        scale[axis, 0:VIEWS, :] = jnp.broadcast_to(1.0 / total, (VIEWS, XY))
    knz[...] = pltpu.roll(kn[2], XY - REACH, 1)

    def toeplitz(view, axis, places):
        result = [jnp.zeros(place.shape, F32) for place in places]
        for tap in range(TAPS):
            value = psf_s[view, axis, tap]
            result = [jnp.where(p == tap, value, r) for p, r in zip(places, result)]
        factor = scale[axis, pl.ds(view, 1), :]
        return [r * factor for r in result]

    def build(begin, end):
        @pl.loop(begin, end)
        def _(view):
            row, lane = iota((16, XY), 0), iota((16, XY), 1)
            lane_x, lane_y = lane // SY, lane % SY
            x_to = [REACH + SX * d + lane_x - row for d in x_shift]
            x_from = [REACH + SX * d + row - lane_x for d in x_shift]
            y_to = [REACH + SY * d + lane_y - row for d in y_shift]
            y_from = [REACH + SY * d + row - lane_y for d in y_shift]
            xs = toeplitz(view, 0, x_to + x_from)
            ys = toeplitz(view, 1, y_to + y_from)
            for x in range(xslots):
                for y in range(3):
                    base = (3 * x + y) * XY
                    for i in range(16):
                        high, low = split(ys[y] * xs[x][i : i + 1, :])
                        kron_h[view, i * 16 : (i + 1) * 16, base : base + XY] = high
                        kron_l[view, i * 16 : (i + 1) * 16, base : base + XY] = low
                        high, low = split(ys[3 + y] * xs[xslots + x][i : i + 1, :])
                        kront_h[view, base + i * 16 : base + (i + 1) * 16, :] = high
                        kront_l[view, base + i * 16 : base + (i + 1) * 16, :] = low
            line = jnp.broadcast_to(knz[pl.ds(view, 1), :], (SZ, ROWS))
            band = pltpu.roll(line, 0, 1, stride=1, stride_axis=0)
            fz[view, 0:SZ], fz[view, SZ : 2 * SZ] = split(band)
            columns = pl.ds(pl.multiple_of(view * SZ, SZ), SZ)
            turned = band.T
            turned = jnp.concatenate([turned[0:GAP], turned[LOW:ROWS]], axis=0)
            bz[0:WIDE, columns], bz[WIDE : 2 * WIDE, columns] = split(turned)

    build(0, 2)
    arrive(est_x)
    for x in range(1, xslots):
        start(est_y[x])
    start(cov_y)
    build(2, 4)
    arrive(raw_ax)

    @pl.loop(0, half)
    def _(view):
        ry_a[view, :, 8:24, :] = rx_a[view, pl.ds(OFF + offsets[0, view], SX), :, :]

    start(raw_ay)

    def turned_y(ry, view, offset):
        return pltpu.roll(ry[view], lax.rem(32 - OFF - offset, 32), 1)[:, 0:SY, :]

    arrive(raw_by)

    @pl.loop(0, half)
    def _(view):
        rx_b[view, 8:24] = turned_y(ry_b, view, offsets[1, half + view])

    start(raw_bx)
    for copies in est_y:
        arrive(copies)
    arrive(cov_y)
    start(est_z)
    build(4, VIEWS)
    arrive(est_z)

    wide_h[...], wide_l[...] = split(wide[...])

    def forward(begin, end):
        @pl.loop(begin, end)
        def _(view):
            total = jnp.zeros((SZ, XY), F32)
            for x in range(xslots):
                cut = slice(x * group, (x + 1) * group)
                part = dot3(fz[view], wide_h[:, cut], wide_l[:, cut])
                stack = jnp.concatenate(split(part), axis=0)
                total = total + dot3(stack, kront_h[view, cut, :], kront_l[view, cut, :])
            blurred[view] = total

    forward(0, 4)
    arrive(raw_ay)
    arrive(raw_bx)

    @pl.loop(0, half)
    def _(view):
        rz[view, 8:136, :] = turned_y(ry_a, view, offsets[1, view]).reshape(XY, SZ).T
        shifted = rx_b[view, pl.ds(OFF + offsets[0, half + view], SX), :, :]
        rz[half + view, 8:136, :] = shifted.reshape(XY, SZ).T

    start(raw_z)
    forward(4, VIEWS)
    arrive(raw_z)

    @pl.loop(0, VIEWS)
    def _(view):
        turn = lax.rem(SZ + 16 - OFF - offsets[2, view], SZ + 16)
        observed = pltpu.roll(rz[view], turn, 0)[0:SZ, :]
        mask = coverage[0, view].astype(F32)
        ratio[view, 0:SZ], ratio[view, SZ : 2 * SZ] = split(mask * observed / blurred[view])

    back_y = [
        [
            to_left("by", spread.at[:, block(x, 1)], from_y.at[1, x]),
            to_right("by", spread.at[:, block(x, 2)], from_y.at[0, x]),
        ]
        for x in range(xslots)
    ]
    back_x = [
        to_left("bx", spread.at[:, block(x_left_slot, 0)], from_x.at[1]),
        to_right("bx", spread.at[:, block(x_right_slot, 0)], from_x.at[0]),
    ]
    back_z = [
        to_left("bz", spread.at[GAP:WIDE, block(0, 0)], from_z.at[1]),
        to_right("bz", spread.at[HIGH:GAP, block(0, 0)], from_z.at[0]),
    ]

    def add_y(x):
        arrive(back_y[x])
        spread[:, block(x, 0)] = spread[:, block(x, 0)] + (from_y[0, x] + from_y[1, x])

    for x in reversed(range(xslots)):
        cut = slice(x * group, (x + 1) * group)

        @pl.loop(0, VIEWS)
        def _(view):
            part = dot3(ratio[view], kron_h[view, :, cut], kron_l[view, :, cut])
            rows_of = pl.ds(pl.multiple_of(view * SZ, SZ), SZ)
            back_h[rows_of, :], back_l[rows_of, :] = split(part)

        for y in (1, 2, 0):
            local = slice(y * XY, (y + 1) * XY)
            spread[:, block(x, y)] = dot3(bz[...], back_h[:, local], back_l[:, local])
            if y > 0:
                start(back_y[x][y - 1 : y])
    for x in range(1, xslots):
        add_y(x)
    start(back_x)

    highest = lax.Precision.HIGHEST
    tap, lane = iota((XY, XY), 0), iota((XY, XY), 1)
    lane_x, lane_y = lane // SY, lane % SY

    def factor(axis, position, shift, size):
        cell = position + REACH - tap[:, : position.shape[1]] - shift * size
        inside = ((cell >= 0) & (cell < size)).astype(F32)
        return jnp.dot(kn[axis], inside, precision=highest, preferred_element_type=F32)

    factor_x = [factor(0, lane_x, d, SX) for d in x_shift]
    factor_y = [factor(1, lane_y, d, SY) for d in y_shift]
    factor_z = [factor(2, lane[:, :SZ], d, SZ) for d in (-1, 0, 1)]
    rows = []
    for z in range(3):
        total = jnp.zeros((8, XY), F32)
        for y in range(3):
            part = jnp.zeros((8, XY), F32)
            for x in range(xslots):
                part = part + jnp.concatenate([cov[z, y, x]] * 2, axis=1) * factor_x[x]
            total = total + part * factor_y[y]
        rows.append(total)
    weights[...] = jnp.dot(
        jnp.concatenate(factor_z, axis=0).T, jnp.concatenate(rows, axis=0),
        precision=highest, preferred_element_type=F32,
    )

    add_y(0)
    arrive(back_x)
    spread[:, block(0, 0)] = spread[:, block(0, 0)] + (from_x[0] + from_x[1])
    start(back_z)
    arrive(back_z)
    total = spread[own, block(0, 0)]
    total = jnp.concatenate(
        [total[0:16] + from_z[0], total[16 : SZ - 16], total[SZ - 16 : SZ] + from_z[1]], axis=0
    )
    restored = wide[own, block(0, 0)] * total / weights[...]
    out[...] = restored.T.reshape(SX, SY, SZ)
    for copies in [est_x, *est_y, cov_y, est_z, raw_ax, raw_ay, raw_bx, raw_by, raw_z]:
        sent(copies)
    for copies in [*back_y, back_x, back_z]:
        sent(copies)


def on_device(counts, estimate, raw_views, psf, offsets, coverage):
    xslots = 2 if counts[0] == 2 else 3
    group = 3 * XY
    lanes = xslots * group
    vmem = pl.BlockSpec(memory_space=pltpu.VMEM)
    smem = pl.BlockSpec(memory_space=pltpu.SMEM)
    return pl.pallas_call(
        functools.partial(kernel, counts),
        out_shape=jax.ShapeDtypeStruct(estimate.shape, F32),
        in_specs=[vmem, vmem, smem, vmem, smem, smem],
        out_specs=vmem,
        scratch_shapes=[
            pltpu.VMEM((ROWS, lanes), F32),
            pltpu.VMEM((ROWS, lanes), BF16),
            pltpu.VMEM((ROWS, lanes), BF16),
            pltpu.VMEM((3, 3, xslots, 8, SZ), F32),
            pltpu.VMEM((VIEWS // 2, 32, SY, SZ), F32),
            pltpu.VMEM((VIEWS // 2, 32, SY, SZ), F32),
            pltpu.VMEM((VIEWS // 2, SX, 32, SZ), F32),
            pltpu.VMEM((VIEWS // 2, SX, 32, SZ), F32),
            pltpu.VMEM((VIEWS, SZ + 16, XY), F32),
            pltpu.VMEM((3, 8, XY), F32),
            pltpu.VMEM((8, XY), F32),
            pltpu.VMEM((3, 8, XY), F32),
            pltpu.VMEM((VIEWS, XY, lanes), BF16),
            pltpu.VMEM((VIEWS, XY, lanes), BF16),
            pltpu.VMEM((VIEWS, lanes, XY), BF16),
            pltpu.VMEM((VIEWS, lanes, XY), BF16),
            pltpu.VMEM((VIEWS, 2 * SZ, ROWS), BF16),
            pltpu.VMEM((2 * WIDE, VIEWS * SZ), BF16),
            pltpu.VMEM((VIEWS, SZ, XY), F32),
            pltpu.VMEM((VIEWS, 2 * SZ, XY), BF16),
            pltpu.VMEM((VIEWS * SZ, group), BF16),
            pltpu.VMEM((VIEWS * SZ, group), BF16),
            pltpu.VMEM((WIDE, lanes), F32),
            pltpu.VMEM((2, WIDE, XY), F32),
            pltpu.VMEM((2, xslots, WIDE, XY), F32),
            pltpu.VMEM((2, 16, XY), F32),
            pltpu.VMEM((SZ, XY), F32),
            pltpu.SemaphoreType.DMA((SEMAPHORES,)),
            pltpu.SemaphoreType.DMA((SEMAPHORES,)),
        ],
        compiler_params=pltpu.CompilerParams(
            collective_id=0, has_side_effects=True, vmem_limit_bytes=56 * 1024 * 1024
        ),
    )(
        estimate, raw_views, psf, psf, offsets.T,
        coverage.transpose(1, 2, 3, 0).reshape(1, VIEWS),
    )


def solution(mesh):
    counts = (mesh.shape["bx"], mesh.shape["by"], mesh.shape["bz"])
    return jax.shard_map(
        functools.partial(on_device, counts),
        mesh=mesh,
        in_specs=(
            P("bx", "by", "bz"),
            P(None, "bx", "by", "bz"),
            P(),
            P(),
            P(None, "bx", "by", "bz"),
        ),
        out_specs=P("bx", "by", "bz"),
        check_vma=False,
    )
```

time: 54.9 us -> 48.4 us (0.88)
  Pallas kernels: 51.1 us -> 46.7 us
  local copies, waits for them, and re-layouts: 3.59 us -> 1.57 us
    pallas_call x1, Pallas kernels: 51.1 us -> 46.7 us  [on_device(): pl.pallas_call(functools.partial(kernel, counts), out_shape=jax.ShapeDtyp...]
    unnamed x5 -> x1, local copies, waits for them, and re-layouts: 3.59 us -> 1.57 us
where the time goes in v1:
time: 48.4 us; the launch traced here: 48.3 us
  Pallas kernels  46.7 us (96%)
  local copies, waits for them, and re-layouts  1.57 us (3%)
    pallas_call x1, Pallas kernels, on_device(): pl.pallas_call(functools.partial(kernel, counts), out_shape=jax.ShapeDtyp...  46.7 us
    unnamed x1, local copies, waits for them, and re-layouts  1.57 us

profile of v1, /device:TPU:1, one launch (start us, length us, event | category | flops | bytes accessed | tf_op | source)
XLA Modules:
  0.0 48.3 jit_solution(5723573437537406966)
XLA Ops:
  0.0 46.7 %shard_map.55 = f32[16,16,128]{2,1,0:T(8,128)} custom-call(f32[16,16,128]{2,1,0:T(8,128)} %est.1, f32[6,16,16,128]{3,2,1,0:T(8,128)} %raw.1, f32[6,3,31]{2,1,0:T(4,128)} %psf_v.1, f32[6,3,31]{2,1,0:T(4,128)} %psf_v.1, s32[3,6]{1,0:T(4,128)} %bitcast.2, s32[1,6]{1,0:T(1,128)} %bitcast.3), custom_call_target="tpu_custom_call" | custom-call | tf_op jit(solution)/shard_map/pallas_call | solution.py:407
  46.7 1.6 %copy.7 = f32[16,16,128]{2,1,0:T(8,128)} copy(f32[16,16,128]{2,1,0:T(8,128)} %shard_map.55) | data formatting | bytes 262144

commit v2 on v1

v2 whole, which is shorter than its diff:
```python
import functools

import jax
import jax.numpy as jnp
from jax import lax
from jax.experimental import pallas as pl
from jax.experimental.pallas import tpu as pltpu
from jax.sharding import PartitionSpec as P

F32 = jnp.float32
BF16 = jnp.bfloat16
MESH = pl.DeviceIdType.MESH
OFF = 8
TAPS = 31
REACH = 15
VIEWS = 6
SEMAPHORES = 48
SX = 16
SY = 16
SZ = 128
XY = SX * SY
LOW, HIGH, WIDE, ROWS = 16, SZ + 16, SZ + 32, 256


def split(value):
    high = value.astype(BF16)
    return high, (value - high.astype(F32)).astype(BF16)


def dot(a, b):
    return jnp.dot(a, b, preferred_element_type=F32)


def iota(shape, dim):
    return lax.broadcasted_iota(jnp.int32, shape, dim)


def dot3(stack, b_high, b_low):
    half = stack.shape[0] // 2
    both = dot(stack, b_high)
    return both[:half] + (both[half:] + dot(stack[:half], b_low))


def kernel(
    counts, est, raw, psf_v, offsets, coverage, out,
    wide, wide_h, wide_l, cov, rx_a, rx_b, ry_a, ry_b, rz_a, rz_b, kn, knz, patterns,
    kron_h, kron_l, kront_h, kront_l, fz, bz,
    blurred, ratio, back_h, back_l, spread, from_x, from_y, from_z, weights, send, recv,
):
    nx, ny, nz = counts
    xslots = 2 if nx == 2 else 3
    group = 3 * XY
    lanes = xslots * group
    ix, iy, iz = lax.axis_index("bx"), lax.axis_index("by"), lax.axis_index("bz")
    where = {"bx": (ix, nx), "by": (iy, ny), "bz": (iz, nz)}
    has_left = {name: i > 0 for name, (i, n) in where.items()}
    has_right = {name: i < n - 1 for name, (i, n) in where.items()}
    x_shift = [0, 1 - 2 * ix] if nx == 2 else [0, -1, 1]
    y_shift = [0, -1, 1]
    x_left_slot = 1
    x_right_slot = 1 if nx == 2 else 2
    used = iter(range(SEMAPHORES))

    def to_side(axis, left, src, dst):
        index = next(used)
        return axis, left, pltpu.make_async_remote_copy(
            src_ref=src, dst_ref=dst, send_sem=send.at[index], recv_sem=recv.at[index],
            device_id={axis: where[axis][0] + (-1 if left else 1)}, device_id_type=MESH,
        )

    def to_left(axis, src, dst):
        return to_side(axis, True, src, dst)

    def to_right(axis, src, dst):
        return to_side(axis, False, src, dst)

    def start(copies):
        for axis, left, copy in copies:
            @pl.when(has_left[axis] if left else has_right[axis])
            def _():
                copy.start()

    def arrive(copies):
        for axis, left, copy in copies:
            @pl.when(has_right[axis] if left else has_left[axis])
            def _():
                copy.wait_recv()

    def sent(copies):
        for axis, left, copy in copies:
            @pl.when(has_left[axis] if left else has_right[axis])
            def _():
                copy.wait_send()

    def absent(axis, left, ref, index):
        @pl.when(jnp.logical_not(has_left[axis] if left else has_right[axis]))
        def _():
            ref[index] = jnp.zeros(ref.at[index].shape, ref.dtype)

    def block(x, y):
        return slice((3 * x + y) * XY, (3 * x + y + 1) * XY)

    full = slice(None)
    own = slice(LOW, HIGH)

    barrier = pltpu.get_barrier_semaphore()
    for axis, (i, n) in where.items():
        @pl.when(has_left[axis])
        def _():
            pl.semaphore_signal(barrier, inc=1, device_id={axis: i - 1}, device_id_type=MESH)

        @pl.when(has_right[axis])
        def _():
            pl.semaphore_signal(barrier, inc=1, device_id={axis: i + 1}, device_id_type=MESH)

    wide[own, block(0, 0)] = est[...].reshape(XY, SZ).T
    cov_rows = jnp.zeros((8, SZ), F32)
    for view in range(VIEWS):
        value = coverage[0, view].astype(F32)
        cov_rows = jnp.where(iota((8, SZ), 0) == view, value, cov_rows)
    cov[0, 0, 1] = cov_rows

    degree = sum(
        (has_left[axis].astype(jnp.int32) + has_right[axis].astype(jnp.int32) for axis in where),
        jnp.int32(0),
    )
    pl.semaphore_wait(barrier, degree)

    half = VIEWS // 2
    first, last = slice(0, half), slice(half, VIEWS)
    est_z = [
        to_left("bz", wide.at[LOW : LOW + 16, block(0, 0)], wide.at[HIGH:WIDE, block(0, 0)]),
        to_right("bz", wide.at[HIGH - 16 : HIGH, block(0, 0)], wide.at[0:LOW, block(0, 0)]),
        to_left("bz", cov.at[0, 0, 1], cov.at[0, 0, 2]),
        to_right("bz", cov.at[0, 0, 1], cov.at[0, 0, 0]),
    ]
    est_x = [
        to_left("bx", wide.at[:, block(0, 0)], wide.at[:, block(x_right_slot, 0)]),
        to_right("bx", wide.at[:, block(0, 0)], wide.at[:, block(x_left_slot, 0)]),
        to_left("bx", cov.at[0, 0], cov.at[0, x_right_slot]),
        to_right("bx", cov.at[0, 0], cov.at[0, x_left_slot]),
    ]
    est_y = [
        [
            to_left("by", wide.at[:, block(x, 0)], wide.at[:, block(x, 2)]),
            to_right("by", wide.at[:, block(x, 0)], wide.at[:, block(x, 1)]),
        ]
        for x in range(xslots)
    ]
    cov_y = [
        to_left("by", cov.at[0], cov.at[2]),
        to_right("by", cov.at[0], cov.at[1]),
    ]
    raw_ax = [
        to_left("bx", raw.at[first, 0:8], rx_a.at[:, 24:32]),
        to_right("bx", raw.at[first, 8:16], rx_a.at[:, 0:8]),
    ]
    raw_ay = [
        to_left("by", ry_a.at[:, :, 8:16], ry_a.at[:, :, 24:32]),
        to_right("by", ry_a.at[:, :, 16:24], ry_a.at[:, :, 0:8]),
    ]
    raw_by = [
        to_left("by", raw.at[last, :, 0:8], ry_b.at[:, :, 24:32]),
        to_right("by", raw.at[last, :, 8:16], ry_b.at[:, :, 0:8]),
    ]
    raw_bx = [
        to_left("bx", rx_b.at[:, 8:16], rx_b.at[:, 24:32]),
        to_right("bx", rx_b.at[:, 16:24], rx_b.at[:, 0:8]),
    ]
    raw_az, raw_bz = [
        [
            to_left("bz", rz.at[:, 8:16], rz.at[:, 136:144]),
            to_right("bz", rz.at[:, 128:136], rz.at[:, 0:8]),
        ]
        for rz in (rz_a, rz_b)
    ]

    start(est_z)
    start(raw_ax)
    start(raw_by)

    blank = jnp.zeros((ROWS - WIDE, lanes), BF16)
    wide_h[WIDE:ROWS, :] = blank
    wide_l[WIDE:ROWS, :] = blank
    if nx > 2:
        for left, slot in ((True, x_left_slot), (False, x_right_slot)):
            absent("bx", left, wide, (full, block(slot, 0)))
            absent("bx", left, cov, (0, slot, full, full, full))
    for left, slot in ((True, 1), (False, 2)):
        for x in range(xslots):
            absent("by", left, wide, (full, block(x, slot)))
        absent("by", left, cov, (slot, full, full, full, full))
    absent("bz", True, wide, (slice(0, LOW), block(0, 0)))
    absent("bz", False, wide, (slice(HIGH, WIDE), block(0, 0)))
    absent("bz", True, cov, (0, 0, 0, full, full))
    absent("bz", False, cov, (0, 0, 2, full, full))
    for rx, ry in ((rx_a, ry_a), (rx_b, ry_b)):
        absent("bx", True, rx, (full, slice(0, 8), full, full))
        absent("bx", False, rx, (full, slice(24, 32), full, full))
        absent("by", True, ry, (full, full, slice(0, 8), full))
        absent("by", False, ry, (full, full, slice(24, 32), full))
    for rz in (rz_a, rz_b):
        absent("bz", True, rz, (full, slice(0, 8), full))
        absent("bz", False, rz, (full, slice(136, 144), full))
    absent("bz", True, from_z, (0, full, full))
    absent("bz", False, from_z, (1, full, full))
    absent("by", True, from_y, (0, full, full, full))
    absent("by", False, from_y, (1, full, full, full))
    absent("bx", True, from_x, (0, full, full))
    absent("bx", False, from_x, (1, full, full))
    rx_a[:, 8:24] = raw[first]
    ry_b[:, :, 8:24] = raw[last]

    kn[...] = jnp.zeros(kn.shape, F32)
    for axis in range(3):
        values = psf_v[:, axis, :]
        kn[axis, 0:VIEWS, 0:TAPS] = values / jnp.sum(values, axis=1, keepdims=True)
    knz[...] = pltpu.roll(kn[2], 1, 1)

    highest = lax.Precision.HIGHEST
    row, lane = iota((XY, XY), 0), iota((XY, XY), 1)
    lane_x, lane_y = lane // SY, lane % SY
    mirror = (row + lane == TAPS - 1).astype(F32)
    kinds = []
    for flip in (False, True):
        for axis, cell, shifts, size in ((0, lane_x, x_shift, SX), (1, lane_y, y_shift, SY)):
            taps = kn[axis]
            if flip:
                taps = jnp.dot(taps, mirror, precision=highest, preferred_element_type=F32)
            taps = pltpu.roll(taps, XY - REACH, 1)
            bands = [
                pltpu.roll(
                    jnp.broadcast_to(taps[view : view + 1, :], (16, XY)), 0, 1, stride=1, stride_axis=0
                )
                for view in range(VIEWS)
            ]
            stack = jnp.concatenate(split(jnp.concatenate(bands, axis=0)), axis=0)
            for shift in shifts:
                place = cell + (-size if flip else size) * shift
                chosen = (row == jnp.where(place < 0, place + XY, place)).astype(BF16)
                both = dot(stack, chosen)
                patterns[len(kinds)] = both[: 16 * VIEWS] + both[16 * VIEWS :]
                kinds.append((flip, axis, shift))
    blur_x, blur_y = 0, xslots
    turn_x, turn_y = xslots + 3, 2 * xslots + 3

    arrive(est_z)
    start(est_x)
    start(est_y[0])

    @pl.loop(0, VIEWS)
    def _(view):
        rows_of = pl.ds(pl.multiple_of(view * 16, 16), 16)
        for x in range(xslots):
            to_x, from_x_row = patterns[blur_x + x, rows_of, :], patterns[turn_x + x, rows_of, :]
            for y in range(3):
                to_y, from_y_row = patterns[blur_y + y, rows_of, :], patterns[turn_y + y, rows_of, :]
                base = (3 * x + y) * XY
                for i in range(16):
                    high, low = split(to_y * to_x[i : i + 1, :])
                    kron_h[view, i * 16 : (i + 1) * 16, base : base + XY] = high
                    kron_l[view, i * 16 : (i + 1) * 16, base : base + XY] = low
                    high, low = split(from_y_row * from_x_row[i : i + 1, :])
                    kront_h[view, base + i * 16 : base + (i + 1) * 16, :] = high
                    kront_l[view, base + i * 16 : base + (i + 1) * 16, :] = low
        line = jnp.broadcast_to(knz[pl.ds(view, 1), :], (SZ, ROWS))
        band = pltpu.roll(line, 0, 1, stride=1, stride_axis=0)
        fz[view, 0:SZ], fz[view, SZ : 2 * SZ] = split(band)
        columns = pl.ds(pl.multiple_of(view * SZ, SZ), SZ)
        bz[0:WIDE, columns], bz[WIDE : 2 * WIDE, columns] = split(band.T[0:WIDE])

    def forward(x, begin, end):
        cut = slice((3 * x + begin) * XY, (3 * x + end) * XY)
        wide_h[0:WIDE, cut], wide_l[0:WIDE, cut] = split(wide[:, cut])

        @pl.loop(0, VIEWS, step=2)
        def _(pair):
            for view in (pair, pair + 1):
                part = dot3(fz[view], wide_h[:, cut], wide_l[:, cut])
                stack = jnp.concatenate(split(part), axis=0)
                part = dot3(stack, kront_h[view, cut, :], kront_l[view, cut, :])
                if x == 0 and begin == 0:
                    blurred[view] = part
                else:
                    blurred[view] = blurred[view] + part

    def turned_y(ry, view, offset):
        return pltpu.roll(ry[view], lax.rem(32 - OFF - offset, 32), 1)[:, 0:SY, :]

    arrive(raw_by)

    @pl.loop(0, half)
    def _(view):
        rx_b[view, 8:24] = turned_y(ry_b, view, offsets[1, half + view])

    start(raw_bx)
    arrive(raw_ax)

    @pl.loop(0, half)
    def _(view):
        ry_a[view, :, 8:24, :] = rx_a[view, pl.ds(OFF + offsets[0, view], SX), :, :]

    start(raw_ay)
    forward(0, 0, 1)
    arrive(est_x)
    for x in range(1, xslots):
        start(est_y[x])
    start(cov_y)
    for x in range(1, xslots):
        forward(x, 0, 1)
    arrive(est_y[0])
    forward(0, 1, 3)
    arrive(raw_bx)

    @pl.loop(0, half)
    def _(view):
        shifted = rx_b[view, pl.ds(OFF + offsets[0, half + view], SX), :, :]
        rz_b[view, 8:136, :] = shifted.reshape(XY, SZ).T

    start(raw_bz)
    for x in range(1, xslots):
        arrive(est_y[x])
        forward(x, 1, 3)
    arrive(raw_ay)

    @pl.loop(0, half)
    def _(view):
        rz_a[view, 8:136, :] = turned_y(ry_a, view, offsets[1, view]).reshape(XY, SZ).T

    start(raw_az)

    def make_ratio(rz, base):
        @pl.loop(0, half)
        def _(index):
            view = base + index
            turn = lax.rem(SZ + 16 - OFF - offsets[2, view], SZ + 16)
            observed = pltpu.roll(rz[index], turn, 0)[0:SZ, :]
            mask = coverage[0, view].astype(F32)
            value = mask * observed / blurred[view]
            ratio[view, 0:SZ], ratio[view, SZ : 2 * SZ] = split(value)

    def backward(x, views):
        cut = slice(x * group, (x + 1) * group)
        for view in views:
            part = dot3(ratio[view], kron_h[view, :, cut], kron_l[view, :, cut])
            rows_of = slice(view * SZ, (view + 1) * SZ)
            back_h[rows_of, cut], back_l[rows_of, cut] = split(part)

    arrive(raw_bz)
    make_ratio(rz_b, half)
    for x in range(xslots):
        backward(x, range(half, VIEWS))
    arrive(raw_az)
    make_ratio(rz_a, 0)

    back_y = [
        [
            to_left("by", spread.at[:, block(x, 1)], from_y.at[1, x]),
            to_right("by", spread.at[:, block(x, 2)], from_y.at[0, x]),
        ]
        for x in range(xslots)
    ]
    back_x = [
        to_left("bx", spread.at[:, block(x_left_slot, 0)], from_x.at[1]),
        to_right("bx", spread.at[:, block(x_right_slot, 0)], from_x.at[0]),
    ]
    back_z = [
        to_left("bz", spread.at[0:LOW, block(0, 0)], from_z.at[1]),
        to_right("bz", spread.at[HIGH:WIDE, block(0, 0)], from_z.at[0]),
    ]

    def add_y(x):
        arrive(back_y[x])
        spread[:, block(x, 0)] = spread[:, block(x, 0)] + (from_y[0, x] + from_y[1, x])

    for x in reversed(range(xslots)):
        backward(x, range(half))
        for y in (1, 2, 0):
            spread[:, block(x, y)] = dot3(bz[...], back_h[:, block(x, y)], back_l[:, block(x, y)])
            if y > 0:
                start(back_y[x][y - 1 : y])
    for x in range(1, xslots):
        add_y(x)
    start(back_x)

    arrive(cov_y)

    def factor(axis, position, shift, size):
        cell = position + REACH - row[:, : position.shape[1]] - shift * size
        inside = ((cell >= 0) & (cell < size)).astype(F32)
        return jnp.dot(kn[axis], inside, precision=highest, preferred_element_type=F32)

    factor_x = [factor(0, lane_x, d, SX) for d in x_shift]
    factor_y = [factor(1, lane_y, d, SY) for d in y_shift]
    factor_z = [factor(2, lane[:, :SZ], d, SZ) for d in (-1, 0, 1)]
    rows = []
    for z in range(3):
        total = jnp.zeros((8, XY), F32)
        for y in range(3):
            part = jnp.zeros((8, XY), F32)
            for x in range(xslots):
                part = part + jnp.concatenate([cov[y, x, z]] * 2, axis=1) * factor_x[x]
            total = total + part * factor_y[y]
        rows.append(total)
    weights[...] = jnp.dot(
        jnp.concatenate(factor_z, axis=0).T, jnp.concatenate(rows, axis=0),
        precision=highest, preferred_element_type=F32,
    )

    add_y(0)
    arrive(back_x)
    spread[:, block(0, 0)] = spread[:, block(0, 0)] + (from_x[0] + from_x[1])
    start(back_z)
    arrive(back_z)
    total = spread[own, block(0, 0)]
    total = jnp.concatenate(
        [total[0:16] + from_z[0], total[16 : SZ - 16], total[SZ - 16 : SZ] + from_z[1]], axis=0
    )
    restored = wide[own, block(0, 0)] * total / weights[...]
    out[...] = restored.T.reshape(SX, SY, SZ)
    for copies in [est_x, *est_y, cov_y, est_z, raw_ax, raw_ay, raw_bx, raw_by, raw_az, raw_bz]:
        sent(copies)
    for copies in [*back_y, back_x, back_z]:
        sent(copies)


def on_device(counts, estimate, raw_views, psf, offsets, coverage):
    xslots = 2 if counts[0] == 2 else 3
    group = 3 * XY
    lanes = xslots * group
    vmem = pl.BlockSpec(memory_space=pltpu.VMEM)
    smem = pl.BlockSpec(memory_space=pltpu.SMEM)
    return pl.pallas_call(
        functools.partial(kernel, counts),
        out_shape=jax.ShapeDtypeStruct(estimate.shape, F32),
        in_specs=[vmem, vmem, vmem, smem, smem],
        out_specs=vmem,
        scratch_shapes=[
            pltpu.VMEM((WIDE, lanes), F32),
            pltpu.VMEM((ROWS, lanes), BF16),
            pltpu.VMEM((ROWS, lanes), BF16),
            pltpu.VMEM((3, xslots, 3, 8, SZ), F32),
            pltpu.VMEM((VIEWS // 2, 32, SY, SZ), F32),
            pltpu.VMEM((VIEWS // 2, 32, SY, SZ), F32),
            pltpu.VMEM((VIEWS // 2, SX, 32, SZ), F32),
            pltpu.VMEM((VIEWS // 2, SX, 32, SZ), F32),
            pltpu.VMEM((VIEWS // 2, SZ + 16, XY), F32),
            pltpu.VMEM((VIEWS // 2, SZ + 16, XY), F32),
            pltpu.VMEM((3, 8, XY), F32),
            pltpu.VMEM((8, XY), F32),
            pltpu.VMEM((2 * xslots + 6, 16 * VIEWS, XY), F32),
            pltpu.VMEM((VIEWS, XY, lanes), BF16),
            pltpu.VMEM((VIEWS, XY, lanes), BF16),
            pltpu.VMEM((VIEWS, lanes, XY), BF16),
            pltpu.VMEM((VIEWS, lanes, XY), BF16),
            pltpu.VMEM((VIEWS, 2 * SZ, ROWS), BF16),
            pltpu.VMEM((2 * WIDE, VIEWS * SZ), BF16),
            pltpu.VMEM((VIEWS, SZ, XY), F32),
            pltpu.VMEM((VIEWS, 2 * SZ, XY), BF16),
            pltpu.VMEM((VIEWS * SZ, lanes), BF16),
            pltpu.VMEM((VIEWS * SZ, lanes), BF16),
            pltpu.VMEM((WIDE, lanes), F32),
            pltpu.VMEM((2, WIDE, XY), F32),
            pltpu.VMEM((2, xslots, WIDE, XY), F32),
            pltpu.VMEM((2, 16, XY), F32),
            pltpu.VMEM((SZ, XY), F32),
            pltpu.SemaphoreType.DMA((SEMAPHORES,)),
            pltpu.SemaphoreType.DMA((SEMAPHORES,)),
        ],
        compiler_params=pltpu.CompilerParams(
            collective_id=0, has_side_effects=True, vmem_limit_bytes=56 * 1024 * 1024
        ),
    )(
        estimate, raw_views, psf, offsets.T,
        coverage.transpose(1, 2, 3, 0).reshape(1, VIEWS),
    )


def solution(mesh):
    counts = (mesh.shape["bx"], mesh.shape["by"], mesh.shape["bz"])
    return jax.shard_map(
        functools.partial(on_device, counts),
        mesh=mesh,
        in_specs=(
            P("bx", "by", "bz"),
            P(None, "bx", "by", "bz"),
            P(),
            P(),
            P(None, "bx", "by", "bz"),
        ),
        out_specs=P("bx", "by", "bz"),
        check_vma=False,
    )
```

time: 48.4 us -> 44.8 us (0.926)
  Pallas kernels: 46.7 us -> 43.1 us
    pallas_call x1, Pallas kernels: 46.7 us -> 43.1 us  [on_device(): pl.pallas_call(functools.partial(kernel, counts), out_shape=jax.ShapeDtyp...]
where the time goes in v2:
time: 44.8 us; the launch traced here: 44.7 us
  Pallas kernels  43.1 us (96%)
  local copies, waits for them, and re-layouts  1.57 us (4%)
    pallas_call x1, Pallas kernels, on_device(): pl.pallas_call(functools.partial(kernel, counts), out_shape=jax.ShapeDtyp...  43.1 us
    unnamed x1, local copies, waits for them, and re-layouts  1.57 us

profile of v2, /device:TPU:1, one launch (start us, length us, event | category | flops | bytes accessed | tf_op | source)
XLA Modules:
  0.0 44.7 jit_solution(1588467505500096478)
XLA Ops:
  0.0 43.1 %shard_map.55 = f32[16,16,128]{2,1,0:T(8,128)} custom-call(f32[16,16,128]{2,1,0:T(8,128)} %est.1, f32[6,16,16,128]{3,2,1,0:T(8,128)} %raw.1, f32[6,3,31]{2,1,0:T(4,128)} %psf_v.1, s32[3,6]{1,0:T(4,128)} %bitcast.2, s32[1,6]{1,0:T(1,128)} %bitcast.3), custom_call_target="tpu_custom_call" | custom-call | tf_op jit(solution)/shard_map/pallas_call | solution.py:433
  43.1 1.6 %copy.7 = f32[16,16,128]{2,1,0:T(8,128)} copy(f32[16,16,128]{2,1,0:T(8,128)} %shard_map.55) | data formatting | bytes 262144

commit v3 on v2

--- a/solution.py
+++ b/solution.py
@@ -43,9 +43,9 @@
 
 def kernel(
     counts, est, raw, psf_v, offsets, coverage, out,
-    wide, wide_h, wide_l, cov, rx_a, rx_b, ry_a, ry_b, rz_a, rz_b, kn, knz, patterns,
+    wide, wide_s, cov, rx_a, rx_b, ry_a, ry_b, rz_a, rz_b, kn, knz, patterns,
     kron_h, kron_l, kront_h, kront_l, fz, bz,
-    blurred, ratio, back_h, back_l, spread, from_x, from_y, from_z, weights, send, recv,
+    blurred, back, spread, from_x, from_y, from_z, weights, send, recv,
 ):
     nx, ny, nz = counts
     xslots = 2 if nx == 2 else 3
@@ -179,9 +179,6 @@
     start(raw_ax)
     start(raw_by)
 
-    blank = jnp.zeros((ROWS - WIDE, lanes), BF16)
-    wide_h[WIDE:ROWS, :] = blank
-    wide_l[WIDE:ROWS, :] = blank
     if nx > 2:
         for left, slot in ((True, x_left_slot), (False, x_right_slot)):
             absent("bx", left, wide, (full, block(slot, 0)))
@@ -248,37 +245,48 @@
     start(est_x)
     start(est_y[0])
 
+    def rows_of(view, i):
+        return pl.ds(pl.multiple_of(view * XY + i * 16, 16), 16)
+
+    def pattern(kind, view):
+        return patterns[kind, pl.ds(pl.multiple_of(view * 16, 16), 16), :]
+
     @pl.loop(0, VIEWS)
     def _(view):
-        rows_of = pl.ds(pl.multiple_of(view * 16, 16), 16)
         for x in range(xslots):
-            to_x, from_x_row = patterns[blur_x + x, rows_of, :], patterns[turn_x + x, rows_of, :]
+            to_x = pattern(turn_x + x, view)
             for y in range(3):
-                to_y, from_y_row = patterns[blur_y + y, rows_of, :], patterns[turn_y + y, rows_of, :]
+                to_y = pattern(turn_y + y, view)
                 base = (3 * x + y) * XY
                 for i in range(16):
                     high, low = split(to_y * to_x[i : i + 1, :])
-                    kron_h[view, i * 16 : (i + 1) * 16, base : base + XY] = high
-                    kron_l[view, i * 16 : (i + 1) * 16, base : base + XY] = low
-                    high, low = split(from_y_row * from_x_row[i : i + 1, :])
                     kront_h[view, base + i * 16 : base + (i + 1) * 16, :] = high
                     kront_l[view, base + i * 16 : base + (i + 1) * 16, :] = low
         line = jnp.broadcast_to(knz[pl.ds(view, 1), :], (SZ, ROWS))
         band = pltpu.roll(line, 0, 1, stride=1, stride_axis=0)
         fz[view, 0:SZ], fz[view, SZ : 2 * SZ] = split(band)
-        columns = pl.ds(pl.multiple_of(view * SZ, SZ), SZ)
-        bz[0:WIDE, columns], bz[WIDE : 2 * WIDE, columns] = split(band.T[0:WIDE])
+        bz[view, 0:WIDE], bz[view, WIDE : 2 * WIDE] = split(band.T[0:WIDE])
+
+    def build_adjoint():
+        @pl.loop(0, VIEWS)
+        def _(view):
+            for x in range(xslots):
+                to_x = pattern(blur_x + x, view)
+                for y in range(3):
+                    to_y = pattern(blur_y + y, view)
+                    for i in range(16):
+                        high, low = split(to_y * to_x[i : i + 1, :])
+                        kron_h[rows_of(view, i), block(x, y)] = high
+                        kron_l[rows_of(view, i), block(x, y)] = low
 
     def forward(x, begin, end):
         cut = slice((3 * x + begin) * XY, (3 * x + end) * XY)
-        wide_h[0:WIDE, cut], wide_l[0:WIDE, cut] = split(wide[:, cut])
+        wide_s[0:WIDE, cut], wide_s[WIDE : 2 * WIDE, cut] = split(wide[:, cut])
 
         @pl.loop(0, VIEWS, step=2)
         def _(pair):
             for view in (pair, pair + 1):
-                part = dot3(fz[view], wide_h[:, cut], wide_l[:, cut])
-                stack = jnp.concatenate(split(part), axis=0)
-                part = dot3(stack, kront_h[view, cut, :], kront_l[view, cut, :])
+                part = dot3(wide_s[:, cut], kront_h[view, cut, :], kront_l[view, cut, :])
                 if x == 0 and begin == 0:
                     blurred[view] = part
                 else:
@@ -310,6 +318,7 @@
         forward(x, 0, 1)
     arrive(est_y[0])
     forward(0, 1, 3)
+    build_adjoint()
     arrive(raw_bx)
 
     @pl.loop(0, half)
@@ -329,29 +338,25 @@
 
     start(raw_az)
 
-    def make_ratio(rz, base):
-        @pl.loop(0, half)
-        def _(index):
+    rest = jnp.zeros((ROWS - WIDE, XY), BF16)
+
+    def ratios(rz, base):
+        for index in range(half):
             view = base + index
             turn = lax.rem(SZ + 16 - OFF - offsets[2, view], SZ + 16)
             observed = pltpu.roll(rz[index], turn, 0)[0:SZ, :]
             mask = coverage[0, view].astype(F32)
-            value = mask * observed / blurred[view]
-            ratio[view, 0:SZ], ratio[view, SZ : 2 * SZ] = split(value)
-
-    def backward(x, views):
-        cut = slice(x * group, (x + 1) * group)
-        for view in views:
-            part = dot3(ratio[view], kron_h[view, :, cut], kron_l[view, :, cut])
-            rows_of = slice(view * SZ, (view + 1) * SZ)
-            back_h[rows_of, cut], back_l[rows_of, cut] = split(part)
+            high, low = split(blurred[view])
+            high = jnp.concatenate([high, rest], axis=0)
+            low = jnp.concatenate([low, rest], axis=0)
+            high, low = split(mask * observed / dot3(fz[view], high, low))
+            columns = slice(view * XY, (view + 1) * XY)
+            back[0:WIDE, columns], back[WIDE : 2 * WIDE, columns] = split(dot3(bz[view], high, low))
 
     arrive(raw_bz)
-    make_ratio(rz_b, half)
-    for x in range(xslots):
-        backward(x, range(half, VIEWS))
+    ratios(rz_b, half)
     arrive(raw_az)
-    make_ratio(rz_a, 0)
+    ratios(rz_a, 0)
 
     back_y = [
         [
@@ -374,9 +379,8 @@
         spread[:, block(x, 0)] = spread[:, block(x, 0)] + (from_y[0, x] + from_y[1, x])
 
     for x in reversed(range(xslots)):
-        backward(x, range(half))
         for y in (1, 2, 0):
-            spread[:, block(x, y)] = dot3(bz[...], back_h[:, block(x, y)], back_l[:, block(x, y)])
+            spread[:, block(x, y)] = dot3(back[...], kron_h[:, block(x, y)], kron_l[:, block(x, y)])
             if y > 0:
                 start(back_y[x][y - 1 : y])
     for x in range(1, xslots):
@@ -437,8 +441,7 @@
         out_specs=vmem,
         scratch_shapes=[
             pltpu.VMEM((WIDE, lanes), F32),
-            pltpu.VMEM((ROWS, lanes), BF16),
-            pltpu.VMEM((ROWS, lanes), BF16),
+            pltpu.VMEM((2 * WIDE, lanes), BF16),
             pltpu.VMEM((3, xslots, 3, 8, SZ), F32),
             pltpu.VMEM((VIEWS // 2, 32, SY, SZ), F32),
             pltpu.VMEM((VIEWS // 2, 32, SY, SZ), F32),
@@ -449,16 +452,14 @@
             pltpu.VMEM((3, 8, XY), F32),
             pltpu.VMEM((8, XY), F32),
             pltpu.VMEM((2 * xslots + 6, 16 * VIEWS, XY), F32),
-            pltpu.VMEM((VIEWS, XY, lanes), BF16),
-            pltpu.VMEM((VIEWS, XY, lanes), BF16),
+            pltpu.VMEM((VIEWS * XY, lanes), BF16),
+            pltpu.VMEM((VIEWS * XY, lanes), BF16),
             pltpu.VMEM((VIEWS, lanes, XY), BF16),
             pltpu.VMEM((VIEWS, lanes, XY), BF16),
             pltpu.VMEM((VIEWS, 2 * SZ, ROWS), BF16),
-            pltpu.VMEM((2 * WIDE, VIEWS * SZ), BF16),
-            pltpu.VMEM((VIEWS, SZ, XY), F32),
-            pltpu.VMEM((VIEWS, 2 * SZ, XY), BF16),
-            pltpu.VMEM((VIEWS * SZ, lanes), BF16),
-            pltpu.VMEM((VIEWS * SZ, lanes), BF16),
+            pltpu.VMEM((VIEWS, 2 * WIDE, SZ), BF16),
+            pltpu.VMEM((VIEWS, WIDE, XY), F32),
+            pltpu.VMEM((2 * WIDE, VIEWS * XY), BF16),
             pltpu.VMEM((WIDE, lanes), F32),
             pltpu.VMEM((2, WIDE, XY), F32),
             pltpu.VMEM((2, xslots, WIDE, XY), F32),

time: 44.8 us -> 43.8 us (0.978)
  Pallas kernels: 43.1 us -> 42.1 us
    pallas_call x1, Pallas kernels: 43.1 us -> 42.1 us  [on_device(): pl.pallas_call(functools.partial(kernel, counts), out_shape=jax.ShapeDtyp...]
where the time goes in v3:
time: 43.8 us; the launch traced here: 43.7 us
  Pallas kernels  42.1 us (96%)
  local copies, waits for them, and re-layouts  1.57 us (4%)
    pallas_call x1, Pallas kernels, on_device(): pl.pallas_call(functools.partial(kernel, counts), out_shape=jax.ShapeDtyp...  42.1 us
    unnamed x1, local copies, waits for them, and re-layouts  1.57 us

profile of v3, /device:TPU:1, one launch (start us, length us, event | category | flops | bytes accessed | tf_op | source)
XLA Modules:
  0.0 43.7 jit_solution(13692430476058475634)
XLA Ops:
  0.0 42.1 %shard_map.55 = f32[16,16,128]{2,1,0:T(8,128)} custom-call(f32[16,16,128]{2,1,0:T(8,128)} %est.1, f32[6,16,16,128]{3,2,1,0:T(8,128)} %raw.1, f32[6,3,31]{2,1,0:T(4,128)} %psf_v.1, s32[3,6]{1,0:T(4,128)} %bitcast.2, s32[1,6]{1,0:T(1,128)} %bitcast.3), custom_call_target="tpu_custom_call" | custom-call | tf_op jit(solution)/shard_map/pallas_call | solution.py:437
  42.1 1.6 %copy.7 = f32[16,16,128]{2,1,0:T(8,128)} copy(f32[16,16,128]{2,1,0:T(8,128)} %shard_map.55) | data formatting | bytes 262144

commit v4 on v3

--- a/solution.py
+++ b/solution.py
@@ -45,7 +45,7 @@
     counts, est, raw, psf_v, offsets, coverage, out,
     wide, wide_s, cov, rx_a, rx_b, ry_a, ry_b, rz_a, rz_b, kn, knz, patterns,
     kron_h, kron_l, kront_h, kront_l, fz, bz,
-    blurred, back, spread, from_x, from_y, from_z, weights, send, recv,
+    blurred, part_a, part_b, back, spread, from_x, from_y, from_za, from_zb, weights, send, recv,
 ):
     nx, ny, nz = counts
     xslots = 2 if nx == 2 else 3
@@ -101,7 +101,6 @@
         return slice((3 * x + y) * XY, (3 * x + y + 1) * XY)
 
     full = slice(None)
-    own = slice(LOW, HIGH)
 
     barrier = pltpu.get_barrier_semaphore()
     for axis, (i, n) in where.items():
@@ -113,7 +112,7 @@
         def _():
             pl.semaphore_signal(barrier, inc=1, device_id={axis: i + 1}, device_id_type=MESH)
 
-    wide[own, block(0, 0)] = est[...].reshape(XY, SZ).T
+    wide[:, block(0, 0)] = est[...].reshape(XY, SZ).T
     cov_rows = jnp.zeros((8, SZ), F32)
     for view in range(VIEWS):
         value = coverage[0, view].astype(F32)
@@ -128,15 +127,15 @@
 
     half = VIEWS // 2
     first, last = slice(0, half), slice(half, VIEWS)
-    est_z = [
-        to_left("bz", wide.at[LOW : LOW + 16, block(0, 0)], wide.at[HIGH:WIDE, block(0, 0)]),
-        to_right("bz", wide.at[HIGH - 16 : HIGH, block(0, 0)], wide.at[0:LOW, block(0, 0)]),
-        to_left("bz", cov.at[0, 0, 1], cov.at[0, 0, 2]),
-        to_right("bz", cov.at[0, 0, 1], cov.at[0, 0, 0]),
-    ]
     est_x = [
         to_left("bx", wide.at[:, block(0, 0)], wide.at[:, block(x_right_slot, 0)]),
         to_right("bx", wide.at[:, block(0, 0)], wide.at[:, block(x_left_slot, 0)]),
+    ]
+    cov_z = [
+        to_left("bz", cov.at[0, 0, 1], cov.at[0, 0, 2]),
+        to_right("bz", cov.at[0, 0, 1], cov.at[0, 0, 0]),
+    ]
+    cov_x = [
         to_left("bx", cov.at[0, 0], cov.at[0, x_right_slot]),
         to_right("bx", cov.at[0, 0], cov.at[0, x_left_slot]),
     ]
@@ -175,9 +174,16 @@
         for rz in (rz_a, rz_b)
     ]
 
-    start(est_z)
+    mid_z = [
+        to_left("bz", blurred.at[:, LOW : LOW + 16], blurred.at[:, HIGH:WIDE]),
+        to_right("bz", blurred.at[:, HIGH - 16 : HIGH], blurred.at[:, 0:LOW]),
+    ]
+
+    start(est_x)
+    start(est_y[0])
+    start(cov_z)
+    start(raw_by)
     start(raw_ax)
-    start(raw_by)
 
     if nx > 2:
         for left, slot in ((True, x_left_slot), (False, x_right_slot)):
@@ -187,8 +193,8 @@
         for x in range(xslots):
             absent("by", left, wide, (full, block(x, slot)))
         absent("by", left, cov, (slot, full, full, full, full))
-    absent("bz", True, wide, (slice(0, LOW), block(0, 0)))
-    absent("bz", False, wide, (slice(HIGH, WIDE), block(0, 0)))
+    absent("bz", True, blurred, (full, slice(0, LOW), full))
+    absent("bz", False, blurred, (full, slice(HIGH, WIDE), full))
     absent("bz", True, cov, (0, 0, 0, full, full))
     absent("bz", False, cov, (0, 0, 2, full, full))
     for rx, ry in ((rx_a, ry_a), (rx_b, ry_b)):
@@ -199,8 +205,9 @@
     for rz in (rz_a, rz_b):
         absent("bz", True, rz, (full, slice(0, 8), full))
         absent("bz", False, rz, (full, slice(136, 144), full))
-    absent("bz", True, from_z, (0, full, full))
-    absent("bz", False, from_z, (1, full, full))
+    for from_z in (from_za, from_zb):
+        absent("bz", True, from_z, (0, full, full, full))
+        absent("bz", False, from_z, (1, full, full, full))
     absent("by", True, from_y, (0, full, full, full))
     absent("by", False, from_y, (1, full, full, full))
     absent("bx", True, from_x, (0, full, full))
@@ -241,31 +248,28 @@
     blur_x, blur_y = 0, xslots
     turn_x, turn_y = xslots + 3, 2 * xslots + 3
 
-    arrive(est_z)
-    start(est_x)
-    start(est_y[0])
-
     def rows_of(view, i):
         return pl.ds(pl.multiple_of(view * XY + i * 16, 16), 16)
 
     def pattern(kind, view):
         return patterns[kind, pl.ds(pl.multiple_of(view * 16, 16), 16), :]
 
-    @pl.loop(0, VIEWS)
-    def _(view):
-        for x in range(xslots):
-            to_x = pattern(turn_x + x, view)
-            for y in range(3):
-                to_y = pattern(turn_y + y, view)
-                base = (3 * x + y) * XY
-                for i in range(16):
-                    high, low = split(to_y * to_x[i : i + 1, :])
-                    kront_h[view, base + i * 16 : base + (i + 1) * 16, :] = high
-                    kront_l[view, base + i * 16 : base + (i + 1) * 16, :] = low
-        line = jnp.broadcast_to(knz[pl.ds(view, 1), :], (SZ, ROWS))
-        band = pltpu.roll(line, 0, 1, stride=1, stride_axis=0)
-        fz[view, 0:SZ], fz[view, SZ : 2 * SZ] = split(band)
-        bz[view, 0:WIDE], bz[view, WIDE : 2 * WIDE] = split(band.T[0:WIDE])
+    def build_forward(begin, end):
+        @pl.loop(begin, end)
+        def _(view):
+            for x in range(xslots):
+                to_x = pattern(turn_x + x, view)
+                for y in range(3):
+                    to_y = pattern(turn_y + y, view)
+                    base = (3 * x + y) * XY
+                    for i in range(16):
+                        high, low = split(to_y * to_x[i : i + 1, :])
+                        kront_h[view, base + i * 16 : base + (i + 1) * 16, :] = high
+                        kront_l[view, base + i * 16 : base + (i + 1) * 16, :] = low
+            line = jnp.broadcast_to(knz[pl.ds(view, 1), :], (SZ, ROWS))
+            band = pltpu.roll(line, 0, 1, stride=1, stride_axis=0)
+            fz[view, 0:SZ], fz[view, SZ : 2 * SZ] = split(band)
+            bz[view, 0:WIDE], bz[view, WIDE : 2 * WIDE] = split(band.T[0:WIDE])
 
     def build_adjoint():
         @pl.loop(0, VIEWS)
@@ -281,20 +285,37 @@
 
     def forward(x, begin, end):
         cut = slice((3 * x + begin) * XY, (3 * x + end) * XY)
-        wide_s[0:WIDE, cut], wide_s[WIDE : 2 * WIDE, cut] = split(wide[:, cut])
+        wide_s[0:SZ, cut], wide_s[SZ : 2 * SZ, cut] = split(wide[:, cut])
 
         @pl.loop(0, VIEWS, step=2)
         def _(pair):
             for view in (pair, pair + 1):
                 part = dot3(wide_s[:, cut], kront_h[view, cut, :], kront_l[view, cut, :])
                 if x == 0 and begin == 0:
-                    blurred[view] = part
+                    blurred[view, LOW:HIGH] = part
                 else:
-                    blurred[view] = blurred[view] + part
+                    blurred[view, LOW:HIGH] = blurred[view, LOW:HIGH] + part
 
     def turned_y(ry, view, offset):
         return pltpu.roll(ry[view], lax.rem(32 - OFF - offset, 32), 1)[:, 0:SY, :]
 
+    def turned_z(rz, index, offset):
+        return pltpu.roll(rz[index], lax.rem(SZ + 16 - OFF - offset, SZ + 16), 0)[0:SZ, :]
+
+    build_forward(0, 2)
+    arrive(est_x)
+    for x in range(1, xslots):
+        start(est_y[x])
+    arrive(cov_z)
+    start(cov_x)
+    arrive(raw_ax)
+
+    @pl.loop(0, half)
+    def _(view):
+        shifted = rx_a[view, pl.ds(OFF + offsets[0, view], SX), :, :]
+        rz_a[view, 8:136, :] = shifted.reshape(XY, SZ).T
+
+    start(raw_az)
     arrive(raw_by)
 
     @pl.loop(0, half)
@@ -302,23 +323,22 @@
         rx_b[view, 8:24] = turned_y(ry_b, view, offsets[1, half + view])
 
     start(raw_bx)
-    arrive(raw_ax)
+    build_forward(2, 4)
+    arrive(raw_az)
 
     @pl.loop(0, half)
     def _(view):
-        ry_a[view, :, 8:24, :] = rx_a[view, pl.ds(OFF + offsets[0, view], SX), :, :]
+        shifted = turned_z(rz_a, view, offsets[2, view]).T
+        ry_a[view, :, 8:24, :] = shifted.reshape(SX, SY, SZ)
 
     start(raw_ay)
-    forward(0, 0, 1)
-    arrive(est_x)
-    for x in range(1, xslots):
-        start(est_y[x])
+    arrive(cov_x)
     start(cov_y)
-    for x in range(1, xslots):
+    build_forward(4, VIEWS)
+    for x in range(xslots):
         forward(x, 0, 1)
     arrive(est_y[0])
     forward(0, 1, 3)
-    build_adjoint()
     arrive(raw_bx)
 
     @pl.loop(0, half)
@@ -330,33 +350,51 @@
     for x in range(1, xslots):
         arrive(est_y[x])
         forward(x, 1, 3)
+    start(mid_z)
+    build_adjoint()
+
+    rest = jnp.zeros((ROWS - WIDE, XY), BF16)
+
+    def ratios(index, base, observed, parts):
+        view = base + index
+        mask = coverage[0, view].astype(F32)
+        high, low = split(blurred[view])
+        high = jnp.concatenate([high, rest], axis=0)
+        low = jnp.concatenate([low, rest], axis=0)
+        high, low = split(mask * observed / dot3(fz[view], high, low))
+        parts[index] = dot3(bz[view], high, low)
+
+    back_za, back_zb = [
+        [
+            to_left("bz", parts.at[:, 0:LOW], from_z.at[1]),
+            to_right("bz", parts.at[:, HIGH:WIDE], from_z.at[0]),
+        ]
+        for parts, from_z in ((part_a, from_za), (part_b, from_zb))
+    ]
+
+    def join(index, base, parts, from_z):
+        low = parts[index, LOW : LOW + 16] + from_z[0, index]
+        high = parts[index, HIGH - 16 : HIGH] + from_z[1, index]
+        value = jnp.concatenate([low, parts[index, LOW + 16 : HIGH - 16], high], axis=0)
+        columns = slice((base + index) * XY, (base + index + 1) * XY)
+        back[0:SZ, columns], back[SZ : 2 * SZ, columns] = split(value)
+
+    arrive(mid_z)
+    arrive(raw_bz)
+    for index in range(half):
+        ratios(index, half, turned_z(rz_b, index, offsets[2, half + index]), part_b)
+    start(back_zb)
     arrive(raw_ay)
-
-    @pl.loop(0, half)
-    def _(view):
-        rz_a[view, 8:136, :] = turned_y(ry_a, view, offsets[1, view]).reshape(XY, SZ).T
-
-    start(raw_az)
-
-    rest = jnp.zeros((ROWS - WIDE, XY), BF16)
-
-    def ratios(rz, base):
-        for index in range(half):
-            view = base + index
-            turn = lax.rem(SZ + 16 - OFF - offsets[2, view], SZ + 16)
-            observed = pltpu.roll(rz[index], turn, 0)[0:SZ, :]
-            mask = coverage[0, view].astype(F32)
-            high, low = split(blurred[view])
-            high = jnp.concatenate([high, rest], axis=0)
-            low = jnp.concatenate([low, rest], axis=0)
-            high, low = split(mask * observed / dot3(fz[view], high, low))
-            columns = slice(view * XY, (view + 1) * XY)
-            back[0:WIDE, columns], back[WIDE : 2 * WIDE, columns] = split(dot3(bz[view], high, low))
-
-    arrive(raw_bz)
-    ratios(rz_b, half)
-    arrive(raw_az)
-    ratios(rz_a, 0)
+    for index in range(half):
+        shifted = turned_y(ry_a, index, offsets[1, index])
+        ratios(index, 0, shifted.reshape(XY, SZ).T, part_a)
+    start(back_za)
+    arrive(back_zb)
+    for index in range(half):
+        join(index, half, part_b, from_zb)
+    arrive(back_za)
+    for index in range(half):
+        join(index, 0, part_a, from_za)
 
     back_y = [
         [
@@ -369,11 +407,6 @@
         to_left("bx", spread.at[:, block(x_left_slot, 0)], from_x.at[1]),
         to_right("bx", spread.at[:, block(x_right_slot, 0)], from_x.at[0]),
     ]
-    back_z = [
-        to_left("bz", spread.at[0:LOW, block(0, 0)], from_z.at[1]),
-        to_right("bz", spread.at[HIGH:WIDE, block(0, 0)], from_z.at[0]),
-    ]
-
     def add_y(x):
         arrive(back_y[x])
         spread[:, block(x, 0)] = spread[:, block(x, 0)] + (from_y[0, x] + from_y[1, x])
@@ -414,17 +447,11 @@
     add_y(0)
     arrive(back_x)
     spread[:, block(0, 0)] = spread[:, block(0, 0)] + (from_x[0] + from_x[1])
-    start(back_z)
-    arrive(back_z)
-    total = spread[own, block(0, 0)]
-    total = jnp.concatenate(
-        [total[0:16] + from_z[0], total[16 : SZ - 16], total[SZ - 16 : SZ] + from_z[1]], axis=0
-    )
-    restored = wide[own, block(0, 0)] * total / weights[...]
+    restored = wide[:, block(0, 0)] * spread[:, block(0, 0)] / weights[...]
     out[...] = restored.T.reshape(SX, SY, SZ)
-    for copies in [est_x, *est_y, cov_y, est_z, raw_ax, raw_ay, raw_bx, raw_by, raw_az, raw_bz]:
+    for copies in [est_x, *est_y, cov_x, cov_y, cov_z, mid_z, raw_ax, raw_ay, raw_bx, raw_by, raw_az, raw_bz]:
         sent(copies)
-    for copies in [*back_y, back_x, back_z]:
+    for copies in [*back_y, back_x, back_za, back_zb]:
         sent(copies)
 
 
@@ -440,8 +467,8 @@
         in_specs=[vmem, vmem, vmem, smem, smem],
         out_specs=vmem,
         scratch_shapes=[
-            pltpu.VMEM((WIDE, lanes), F32),
-            pltpu.VMEM((2 * WIDE, lanes), BF16),
+            pltpu.VMEM((SZ, lanes), F32),
+            pltpu.VMEM((2 * SZ, lanes), BF16),
             pltpu.VMEM((3, xslots, 3, 8, SZ), F32),
             pltpu.VMEM((VIEWS // 2, 32, SY, SZ), F32),
             pltpu.VMEM((VIEWS // 2, 32, SY, SZ), F32),
@@ -459,11 +486,14 @@
             pltpu.VMEM((VIEWS, 2 * SZ, ROWS), BF16),
             pltpu.VMEM((VIEWS, 2 * WIDE, SZ), BF16),
             pltpu.VMEM((VIEWS, WIDE, XY), F32),
-            pltpu.VMEM((2 * WIDE, VIEWS * XY), BF16),
-            pltpu.VMEM((WIDE, lanes), F32),
-            pltpu.VMEM((2, WIDE, XY), F32),
-            pltpu.VMEM((2, xslots, WIDE, XY), F32),
-            pltpu.VMEM((2, 16, XY), F32),
+            pltpu.VMEM((VIEWS // 2, WIDE, XY), F32),
+            pltpu.VMEM((VIEWS // 2, WIDE, XY), F32),
+            pltpu.VMEM((2 * SZ, VIEWS * XY), BF16),
+            pltpu.VMEM((SZ, lanes), F32),
+            pltpu.VMEM((2, SZ, XY), F32),
+            pltpu.VMEM((2, xslots, SZ, XY), F32),
+            pltpu.VMEM((2, VIEWS // 2, 16, XY), F32),
+            pltpu.VMEM((2, VIEWS // 2, 16, XY), F32),
             pltpu.VMEM((SZ, XY), F32),
             pltpu.SemaphoreType.DMA((SEMAPHORES,)),
             pltpu.SemaphoreType.DMA((SEMAPHORES,)),

time: 43.8 us -> 41.3 us (0.943)
  Pallas kernels: 42.1 us -> 39.6 us
    pallas_call x1, Pallas kernels: 42.1 us -> 39.6 us  [on_device(): pl.pallas_call(functools.partial(kernel, counts), out_shape=jax.ShapeDtyp...]
where the time goes in v4:
time: 41.3 us; the launch traced here: 41.2 us
  Pallas kernels  39.6 us (96%)
  local copies, waits for them, and re-layouts  1.57 us (4%)
    pallas_call x1, Pallas kernels, on_device(): pl.pallas_call(functools.partial(kernel, counts), out_shape=jax.ShapeDtyp...  39.6 us
    unnamed x1, local copies, waits for them, and re-layouts  1.57 us

profile of v4, /device:TPU:1, one launch (start us, length us, event | category | flops | bytes accessed | tf_op | source)
XLA Modules:
  0.0 41.2 jit_solution(9306612010962973432)
XLA Ops:
  0.0 39.6 %shard_map.55 = f32[16,16,128]{2,1,0:T(8,128)} custom-call(f32[16,16,128]{2,1,0:T(8,128)} %est.1, f32[6,16,16,128]{3,2,1,0:T(8,128)} %raw.1, f32[6,3,31]{2,1,0:T(4,128)} %psf_v.1, s32[3,6]{1,0:T(4,128)} %bitcast.2, s32[1,6]{1,0:T(1,128)} %bitcast.3), custom_call_target="tpu_custom_call" | custom-call | tf_op jit(solution)/shard_map/pallas_call | solution.py:464
  39.6 1.6 %copy.7 = f32[16,16,128]{2,1,0:T(8,128)} copy(f32[16,16,128]{2,1,0:T(8,128)} %shard_map.55) | data formatting | bytes 262144

commit v5 on v4

--- a/solution.py
+++ b/solution.py
@@ -44,7 +44,7 @@
 def kernel(
     counts, est, raw, psf_v, offsets, coverage, out,
     wide, wide_s, cov, rx_a, rx_b, ry_a, ry_b, rz_a, rz_b, kn, knz, patterns,
-    kron_h, kron_l, kront_h, kront_l, fz, bz,
+    kron_h, kron_l, fz, bz,
     blurred, part_a, part_b, back, spread, from_x, from_y, from_za, from_zb, weights, send, recv,
 ):
     nx, ny, nz = counts
@@ -225,31 +225,26 @@
     row, lane = iota((XY, XY), 0), iota((XY, XY), 1)
     lane_x, lane_y = lane // SY, lane % SY
     mirror = (row + lane == TAPS - 1).astype(F32)
-    kinds = []
-    for flip in (False, True):
-        for axis, cell, shifts, size in ((0, lane_x, x_shift, SX), (1, lane_y, y_shift, SY)):
-            taps = kn[axis]
-            if flip:
-                taps = jnp.dot(taps, mirror, precision=highest, preferred_element_type=F32)
-            taps = pltpu.roll(taps, XY - REACH, 1)
-            bands = [
-                pltpu.roll(
-                    jnp.broadcast_to(taps[view : view + 1, :], (16, XY)), 0, 1, stride=1, stride_axis=0
-                )
-                for view in range(VIEWS)
-            ]
-            stack = jnp.concatenate(split(jnp.concatenate(bands, axis=0)), axis=0)
-            for shift in shifts:
-                place = cell + (-size if flip else size) * shift
-                chosen = (row == jnp.where(place < 0, place + XY, place)).astype(BF16)
-                both = dot(stack, chosen)
-                patterns[len(kinds)] = both[: 16 * VIEWS] + both[16 * VIEWS :]
-                kinds.append((flip, axis, shift))
-    blur_x, blur_y = 0, xslots
-    turn_x, turn_y = xslots + 3, 2 * xslots + 3
-
-    def rows_of(view, i):
-        return pl.ds(pl.multiple_of(view * XY + i * 16, 16), 16)
+    kind = 0
+    for axis, cell, shifts, size in ((0, lane_x, x_shift, SX), (1, lane_y, y_shift, SY)):
+        taps = jnp.dot(kn[axis], mirror, precision=highest, preferred_element_type=F32)
+        taps = pltpu.roll(taps, XY - REACH, 1)
+        bands = [
+            pltpu.roll(
+                jnp.broadcast_to(taps[view : view + 1, :], (16, XY)), 0, 1, stride=1, stride_axis=0
+            )
+            for view in range(VIEWS)
+        ]
+        stack = jnp.concatenate(split(jnp.concatenate(bands, axis=0)), axis=0)
+        for shift in shifts:
+            place = cell - size * shift
+            chosen = (row == jnp.where(place < 0, place + XY, place)).astype(BF16)
+            both = dot(stack, chosen)
+            patterns[kind] = both[: 16 * VIEWS] + both[16 * VIEWS :]
+            kind += 1
+
+    def columns_of(view):
+        return pl.ds(pl.multiple_of(view * XY, XY), XY)
 
     def pattern(kind, view):
         return patterns[kind, pl.ds(pl.multiple_of(view * 16, 16), 16), :]
@@ -258,31 +253,19 @@
         @pl.loop(begin, end)
         def _(view):
             for x in range(xslots):
-                to_x = pattern(turn_x + x, view)
+                to_x = pattern(x, view)
                 for y in range(3):
-                    to_y = pattern(turn_y + y, view)
+                    to_y = pattern(xslots + y, view)
                     base = (3 * x + y) * XY
                     for i in range(16):
                         high, low = split(to_y * to_x[i : i + 1, :])
-                        kront_h[view, base + i * 16 : base + (i + 1) * 16, :] = high
-                        kront_l[view, base + i * 16 : base + (i + 1) * 16, :] = low
+                        kron_h[base + i * 16 : base + (i + 1) * 16, columns_of(view)] = high
+                        kron_l[base + i * 16 : base + (i + 1) * 16, columns_of(view)] = low
             line = jnp.broadcast_to(knz[pl.ds(view, 1), :], (SZ, ROWS))
             band = pltpu.roll(line, 0, 1, stride=1, stride_axis=0)
             fz[view, 0:SZ], fz[view, SZ : 2 * SZ] = split(band)
             bz[view, 0:WIDE], bz[view, WIDE : 2 * WIDE] = split(band.T[0:WIDE])
 
-    def build_adjoint():
-        @pl.loop(0, VIEWS)
-        def _(view):
-            for x in range(xslots):
-                to_x = pattern(blur_x + x, view)
-                for y in range(3):
-                    to_y = pattern(blur_y + y, view)
-                    for i in range(16):
-                        high, low = split(to_y * to_x[i : i + 1, :])
-                        kron_h[rows_of(view, i), block(x, y)] = high
-                        kron_l[rows_of(view, i), block(x, y)] = low
-
     def forward(x, begin, end):
         cut = slice((3 * x + begin) * XY, (3 * x + end) * XY)
         wide_s[0:SZ, cut], wide_s[SZ : 2 * SZ, cut] = split(wide[:, cut])
@@ -290,7 +273,8 @@
         @pl.loop(0, VIEWS, step=2)
         def _(pair):
             for view in (pair, pair + 1):
-                part = dot3(wide_s[:, cut], kront_h[view, cut, :], kront_l[view, cut, :])
+                columns = columns_of(view)
+                part = dot3(wide_s[:, cut], kron_h[cut, columns], kron_l[cut, columns])
                 if x == 0 and begin == 0:
                     blurred[view, LOW:HIGH] = part
                 else:
@@ -351,7 +335,6 @@
         arrive(est_y[x])
         forward(x, 1, 3)
     start(mid_z)
-    build_adjoint()
 
     rest = jnp.zeros((ROWS - WIDE, XY), BF16)
 
@@ -376,8 +359,8 @@
         low = parts[index, LOW : LOW + 16] + from_z[0, index]
         high = parts[index, HIGH - 16 : HIGH] + from_z[1, index]
         value = jnp.concatenate([low, parts[index, LOW + 16 : HIGH - 16], high], axis=0)
-        columns = slice((base + index) * XY, (base + index + 1) * XY)
-        back[0:SZ, columns], back[SZ : 2 * SZ, columns] = split(value)
+        rows_of = slice((base + index) * XY, (base + index + 1) * XY)
+        back[rows_of, 0:SZ], back[rows_of, SZ : 2 * SZ] = split(value.T)
 
     arrive(mid_z)
     arrive(raw_bz)
@@ -398,22 +381,24 @@
 
     back_y = [
         [
-            to_left("by", spread.at[:, block(x, 1)], from_y.at[1, x]),
-            to_right("by", spread.at[:, block(x, 2)], from_y.at[0, x]),
+            to_left("by", spread.at[block(x, 1)], from_y.at[1, x]),
+            to_right("by", spread.at[block(x, 2)], from_y.at[0, x]),
         ]
         for x in range(xslots)
     ]
     back_x = [
-        to_left("bx", spread.at[:, block(x_left_slot, 0)], from_x.at[1]),
-        to_right("bx", spread.at[:, block(x_right_slot, 0)], from_x.at[0]),
+        to_left("bx", spread.at[block(x_left_slot, 0)], from_x.at[1]),
+        to_right("bx", spread.at[block(x_right_slot, 0)], from_x.at[0]),
     ]
     def add_y(x):
         arrive(back_y[x])
-        spread[:, block(x, 0)] = spread[:, block(x, 0)] + (from_y[0, x] + from_y[1, x])
+        spread[block(x, 0)] = spread[block(x, 0)] + (from_y[0, x] + from_y[1, x])
 
     for x in reversed(range(xslots)):
         for y in (1, 2, 0):
-            spread[:, block(x, y)] = dot3(back[...], kron_h[:, block(x, y)], kron_l[:, block(x, y)])
+            both = dot(kron_h[block(x, y), :], back[...])
+            low = dot(kron_l[block(x, y), :], back[:, 0:SZ])
+            spread[block(x, y)] = both[:, 0:SZ] + (both[:, SZ : 2 * SZ] + low)
             if y > 0:
                 start(back_y[x][y - 1 : y])
     for x in range(1, xslots):
@@ -440,15 +425,15 @@
             total = total + part * factor_y[y]
         rows.append(total)
     weights[...] = jnp.dot(
-        jnp.concatenate(factor_z, axis=0).T, jnp.concatenate(rows, axis=0),
+        jnp.concatenate(rows, axis=0).T, jnp.concatenate(factor_z, axis=0),
         precision=highest, preferred_element_type=F32,
     )
 
     add_y(0)
     arrive(back_x)
-    spread[:, block(0, 0)] = spread[:, block(0, 0)] + (from_x[0] + from_x[1])
-    restored = wide[:, block(0, 0)] * spread[:, block(0, 0)] / weights[...]
-    out[...] = restored.T.reshape(SX, SY, SZ)
+    total = spread[block(0, 0)] + (from_x[0] + from_x[1])
+    restored = est[...].reshape(XY, SZ) * total / weights[...]
+    out[...] = restored.reshape(SX, SY, SZ)
     for copies in [est_x, *est_y, cov_x, cov_y, cov_z, mid_z, raw_ax, raw_ay, raw_bx, raw_by, raw_az, raw_bz]:
         sent(copies)
     for copies in [*back_y, back_x, back_za, back_zb]:
@@ -478,23 +463,21 @@
             pltpu.VMEM((VIEWS // 2, SZ + 16, XY), F32),
             pltpu.VMEM((3, 8, XY), F32),
             pltpu.VMEM((8, XY), F32),
-            pltpu.VMEM((2 * xslots + 6, 16 * VIEWS, XY), F32),
-            pltpu.VMEM((VIEWS * XY, lanes), BF16),
-            pltpu.VMEM((VIEWS * XY, lanes), BF16),
-            pltpu.VMEM((VIEWS, lanes, XY), BF16),
-            pltpu.VMEM((VIEWS, lanes, XY), BF16),
+            pltpu.VMEM((xslots + 3, 16 * VIEWS, XY), F32),
+            pltpu.VMEM((lanes, VIEWS * XY), BF16),
+            pltpu.VMEM((lanes, VIEWS * XY), BF16),
             pltpu.VMEM((VIEWS, 2 * SZ, ROWS), BF16),
             pltpu.VMEM((VIEWS, 2 * WIDE, SZ), BF16),
             pltpu.VMEM((VIEWS, WIDE, XY), F32),
             pltpu.VMEM((VIEWS // 2, WIDE, XY), F32),
             pltpu.VMEM((VIEWS // 2, WIDE, XY), F32),
-            pltpu.VMEM((2 * SZ, VIEWS * XY), BF16),
-            pltpu.VMEM((SZ, lanes), F32),
-            pltpu.VMEM((2, SZ, XY), F32),
-            pltpu.VMEM((2, xslots, SZ, XY), F32),
+            pltpu.VMEM((VIEWS * XY, 2 * SZ), BF16),
+            pltpu.VMEM((lanes, SZ), F32),
+            pltpu.VMEM((2, XY, SZ), F32),
+            pltpu.VMEM((2, xslots, XY, SZ), F32),
             pltpu.VMEM((2, VIEWS // 2, 16, XY), F32),
             pltpu.VMEM((2, VIEWS // 2, 16, XY), F32),
-            pltpu.VMEM((SZ, XY), F32),
+            pltpu.VMEM((XY, SZ), F32),
             pltpu.SemaphoreType.DMA((SEMAPHORES,)),
             pltpu.SemaphoreType.DMA((SEMAPHORES,)),
         ],

time: 41.3 us -> 41.3 us (level)
  no operation moved by 1% of the time
where the time goes in v5:
time: 41.3 us; the launch traced here: 41.1 us
  Pallas kernels  39.6 us (96%)
  local copies, waits for them, and re-layouts  1.57 us (4%)
    pallas_call x1, Pallas kernels, on_device(): pl.pallas_call(functools.partial(kernel, counts), out_shape=jax.ShapeDtyp...  39.6 us
    unnamed x1, local copies, waits for them, and re-layouts  1.57 us

profile of v5, /device:TPU:1, one launch (start us, length us, event | category | flops | bytes accessed | tf_op | source)
XLA Modules:
  0.0 41.1 jit_solution(10711844567946762871)
XLA Ops:
  0.0 39.6 %shard_map.55 = f32[16,16,128]{2,1,0:T(8,128)} custom-call(f32[16,16,128]{2,1,0:T(8,128)} %est.1, f32[6,16,16,128]{3,2,1,0:T(8,128)} %raw.1, f32[6,3,31]{2,1,0:T(4,128)} %psf_v.1, s32[3,6]{1,0:T(4,128)} %bitcast.2, s32[1,6]{1,0:T(1,128)} %bitcast.3), custom_call_target="tpu_custom_call" | custom-call | tf_op jit(solution)/shard_map/pallas_call | solution.py:449
  39.6 1.6 %copy.7 = f32[16,16,128]{2,1,0:T(8,128)} copy(f32[16,16,128]{2,1,0:T(8,128)} %shard_map.55) | data formatting | bytes 262144

commit v6 on v5

--- a/solution.py
+++ b/solution.py
@@ -45,7 +45,7 @@
     counts, est, raw, psf_v, offsets, coverage, out,
     wide, wide_s, cov, rx_a, rx_b, ry_a, ry_b, rz_a, rz_b, kn, knz, patterns,
     kron_h, kron_l, fz, bz,
-    blurred, part_a, part_b, back, spread, from_x, from_y, from_za, from_zb, weights, send, recv,
+    blurred, part_a, part_b, back, spread, from_x, from_y, from_za, from_zb, weights, send, recv, local,
 ):
     nx, ny, nz = counts
     xslots = 2 if nx == 2 else 3
@@ -212,8 +212,10 @@
     absent("by", False, from_y, (1, full, full, full))
     absent("bx", True, from_x, (0, full, full))
     absent("bx", False, from_x, (1, full, full))
-    rx_a[:, 8:24] = raw[first]
-    ry_b[:, :, 8:24] = raw[last]
+    own_a = pltpu.make_async_copy(raw.at[first], rx_a.at[:, 8:24], local.at[0])
+    own_b = pltpu.make_async_copy(raw.at[last], ry_b.at[:, :, 8:24], local.at[1])
+    own_a.start()
+    own_b.start()
 
     kn[...] = jnp.zeros(kn.shape, F32)
     for axis in range(3):
@@ -292,6 +294,7 @@
         start(est_y[x])
     arrive(cov_z)
     start(cov_x)
+    own_a.wait()
     arrive(raw_ax)
 
     @pl.loop(0, half)
@@ -300,6 +303,7 @@
         rz_a[view, 8:136, :] = shifted.reshape(XY, SZ).T
 
     start(raw_az)
+    own_b.wait()
     arrive(raw_by)
 
     @pl.loop(0, half)
@@ -367,43 +371,6 @@
     for index in range(half):
         ratios(index, half, turned_z(rz_b, index, offsets[2, half + index]), part_b)
     start(back_zb)
-    arrive(raw_ay)
-    for index in range(half):
-        shifted = turned_y(ry_a, index, offsets[1, index])
-        ratios(index, 0, shifted.reshape(XY, SZ).T, part_a)
-    start(back_za)
-    arrive(back_zb)
-    for index in range(half):
-        join(index, half, part_b, from_zb)
-    arrive(back_za)
-    for index in range(half):
-        join(index, 0, part_a, from_za)
-
-    back_y = [
-        [
-            to_left("by", spread.at[block(x, 1)], from_y.at[1, x]),
-            to_right("by", spread.at[block(x, 2)], from_y.at[0, x]),
-        ]
-        for x in range(xslots)
-    ]
-    back_x = [
-        to_left("bx", spread.at[block(x_left_slot, 0)], from_x.at[1]),
-        to_right("bx", spread.at[block(x_right_slot, 0)], from_x.at[0]),
-    ]
-    def add_y(x):
-        arrive(back_y[x])
-        spread[block(x, 0)] = spread[block(x, 0)] + (from_y[0, x] + from_y[1, x])
-
-    for x in reversed(range(xslots)):
-        for y in (1, 2, 0):
-            both = dot(kron_h[block(x, y), :], back[...])
-            low = dot(kron_l[block(x, y), :], back[:, 0:SZ])
-            spread[block(x, y)] = both[:, 0:SZ] + (both[:, SZ : 2 * SZ] + low)
-            if y > 0:
-                start(back_y[x][y - 1 : y])
-    for x in range(1, xslots):
-        add_y(x)
-    start(back_x)
 
     arrive(cov_y)
 
@@ -429,6 +396,45 @@
         precision=highest, preferred_element_type=F32,
     )
 
+    arrive(raw_ay)
+    for index in range(half):
+        shifted = turned_y(ry_a, index, offsets[1, index])
+        ratios(index, 0, shifted.reshape(XY, SZ).T, part_a)
+    start(back_za)
+    arrive(back_zb)
+    for index in range(half):
+        join(index, half, part_b, from_zb)
+    arrive(back_za)
+    for index in range(half):
+        join(index, 0, part_a, from_za)
+
+    back_y = [
+        [
+            to_left("by", spread.at[block(x, 1)], from_y.at[1, x]),
+            to_right("by", spread.at[block(x, 2)], from_y.at[0, x]),
+        ]
+        for x in range(xslots)
+    ]
+    back_x = [
+        to_left("bx", spread.at[block(x_left_slot, 0)], from_x.at[1]),
+        to_right("bx", spread.at[block(x_right_slot, 0)], from_x.at[0]),
+    ]
+    def add_y(x):
+        arrive(back_y[x])
+        spread[block(x, 0)] = spread[block(x, 0)] + (from_y[0, x] + from_y[1, x])
+
+    for x in reversed(range(xslots)):
+        for y in (1, 2, 0):
+            if x == 0 and y == 0:
+                for slot in range(1, xslots):
+                    add_y(slot)
+                start(back_x)
+            both = dot(kron_h[block(x, y), :], back[...])
+            low = dot(kron_l[block(x, y), :], back[:, 0:SZ])
+            spread[block(x, y)] = both[:, 0:SZ] + (both[:, SZ : 2 * SZ] + low)
+            if y > 0:
+                start(back_y[x][y - 1 : y])
+
     add_y(0)
     arrive(back_x)
     total = spread[block(0, 0)] + (from_x[0] + from_x[1])
@@ -449,7 +455,7 @@
     return pl.pallas_call(
         functools.partial(kernel, counts),
         out_shape=jax.ShapeDtypeStruct(estimate.shape, F32),
-        in_specs=[vmem, vmem, vmem, smem, smem],
+        in_specs=[vmem, pl.BlockSpec(memory_space=pl.ANY), vmem, smem, smem],
         out_specs=vmem,
         scratch_shapes=[
             pltpu.VMEM((SZ, lanes), F32),
@@ -480,6 +486,7 @@
             pltpu.VMEM((XY, SZ), F32),
             pltpu.SemaphoreType.DMA((SEMAPHORES,)),
             pltpu.SemaphoreType.DMA((SEMAPHORES,)),
+            pltpu.SemaphoreType.DMA((2,)),
         ],
         compiler_params=pltpu.CompilerParams(
             collective_id=0, has_side_effects=True, vmem_limit_bytes=56 * 1024 * 1024

time: 41.3 us -> 42.6 us (1.031)
  Pallas kernels: 39.6 us -> 40.9 us
    pallas_call x1, Pallas kernels: 39.6 us -> 40.9 us  [on_device(): pl.pallas_call(functools.partial(kernel, counts), out_shape=jax.ShapeDtyp...]
where the time goes in v6:
time: 42.6 us; the launch traced here: 42.5 us
  Pallas kernels  40.9 us (96%)
  local copies, waits for them, and re-layouts  1.57 us (4%)
    pallas_call x1, Pallas kernels, on_device(): pl.pallas_call(functools.partial(kernel, counts), out_shape=jax.ShapeDtyp...  40.9 us
    unnamed x1, local copies, waits for them, and re-layouts  1.57 us

profile of v6, /device:TPU:1, one launch (start us, length us, event | category | flops | bytes accessed | tf_op | source)
XLA Modules:
  0.0 42.5 jit_solution(8441454953900212626)
XLA Ops:
  0.0 40.9 %shard_map.55 = f32[16,16,128]{2,1,0:T(8,128)} custom-call(f32[16,16,128]{2,1,0:T(8,128)} %est.1, f32[6,16,16,128]{3,2,1,0:T(8,128)} %raw.1, f32[6,3,31]{2,1,0:T(4,128)} %psf_v.1, s32[3,6]{1,0:T(4,128)} %bitcast.2, s32[1,6]{1,0:T(1,128)} %bitcast.3), custom_call_target="tpu_custom_call" | custom-call | tf_op jit(solution)/shard_map/pallas_call | solution.py:455
  40.9 1.6 %copy.7 = f32[16,16,128]{2,1,0:T(8,128)} copy(f32[16,16,128]{2,1,0:T(8,128)} %shard_map.55) | data formatting | bytes 262144
